TPU v7x, 32 devices: a whole 2x2x4 slice. The times are simulated.
32 devices in a mesh: expert: 16 (over z, y, x), seq: 2 (over core).
Axes of the slice: x: 2, y: 2, z: 4, core: 2. Of those that a mesh axis runs over, the one named last changes fastest.
Arguments:
- hidden_rows: bfloat16 [2048, 8, 1024], P(('expert', 'seq')), may hold values from -16 to 16
- routes: int32 [2048, 8], P(('expert', 'seq')), may hold values from 0 to 15, all different within a row; in each aligned block of 64 rows (0 to 63, 64 to 127, ...) at most 64 rows name the same one
- down_weight: bfloat16 [16, 7168, 1024], P('expert', 'seq'), may hold values from -0.1875 to 0.1875
- probe: bfloat16 [7168, 256], P('seq'), may hold values from -0.0625 to 0.0625
Outputs:
- basis: float32 [7168, 256], P(('seq', 'expert'))
- coefficients: float32 [16, 256, 1024], P('expert', None, 'seq')
Inputs may be any that keep to these rules, and one draw needn't show every extreme that they name: `routes`: in each aligned block of 64 tokens no expert is named in more than 64 places, and some expert in exactly 64; the 8 experts of a token differ.
All inputs are finite; a program needn't handle non-finite values.
Results may differ from a plain program's by a relative error of at most 0.0054.
Values may be sent and summed in bfloat16 or wider, within the bound.
A program may use at most 64 MiB of HBM per device.

v0:
```python
import jax
import jax.numpy as jnp
from jax import lax
from jax.sharding import PartitionSpec as P


def body(hidden_rows, routes, down_weight, probe):
    weight = down_weight[0]
    tok_count, top_count = routes.shape
    feature_width = hidden_rows.shape[2]
    experts = lax.axis_size("expert")
    capacity = 2 * tok_count * top_count // experts
    row_mean = tok_count * top_count * lax.axis_size("seq")
    partial_value = lax.dot_general(
        weight, probe, (((0,), (0,)), ((), ())), preferred_element_type=jnp.float32
    )
    probe_proj = lax.psum(partial_value, "seq").astype(jnp.bfloat16)
    expert_ids = routes.reshape(-1)
    onehot = (expert_ids[:, None] == jnp.arange(experts, dtype=jnp.int32)[None, :]).astype(
        jnp.int32
    )
    position = jnp.sum(onehot * (jnp.cumsum(onehot, axis=0) - 1), axis=1)
    destination = expert_ids * capacity + position
    outgoing = jnp.zeros((experts * capacity, feature_width), jnp.bfloat16)
    outgoing = outgoing.at[destination].set(hidden_rows.reshape(-1, feature_width))
    outgoing = outgoing.reshape(experts, capacity, feature_width)
    arrived = lax.all_to_all(outgoing, "expert", split_axis=0, concat_axis=0, tiled=True)
    arrived_rows = arrived.reshape(-1, feature_width)
    mixed = jnp.dot(arrived_rows, probe_proj, preferred_element_type=jnp.float32).astype(
        jnp.bfloat16
    )
    gram_part = lax.dot_general(
        arrived_rows, mixed, (((0,), (0,)), ((), ())), preferred_element_type=jnp.float32
    )
    gram_full = lax.psum(gram_part, "seq") / row_mean
    panel_image = jnp.dot(
        weight, gram_full.astype(jnp.bfloat16), preferred_element_type=jnp.float32
    )
    basis_rows = lax.psum_scatter(panel_image, "expert", scatter_dimension=0, tiled=True)
    coef_part = lax.dot_general(
        lax.all_gather(basis_rows.astype(jnp.bfloat16), "expert", axis=0, tiled=True),
        weight,
        (((0,), (0,)), ((), ())),
        preferred_element_type=jnp.float32,
    )
    coefficients = lax.psum_scatter(coef_part, "seq", scatter_dimension=1, tiled=True)
    return (basis_rows, coefficients[None])


def solution(mesh):
    in_specs = (
        P(("expert", "seq"), None, None),
        P(("expert", "seq"), None),
        P("expert", "seq", None),
        P("seq", None),
    )
    out_specs = (P(("seq", "expert"), None), P("expert", None, "seq"))
    return jax.shard_map(body, mesh=mesh, in_specs=in_specs, out_specs=out_specs, check_vma=False)
```

profile of v0, /device:TPU:0, one launch (start us, length us, event | category | flops | bytes accessed | tf_op | source)
XLA Modules:
  0.0 278.3 jit_solution(9031876554945925457)
XLA Ops:
  7.2 0.8 broadcast_multiply_fusion
  8.0 0.8 copy.19
  8.8 0.1 eq.29
  8.9 0.1 eq.25
  9.0 0.1 copy.18
  9.0 0.1 mul.21
  9.1 1.2 reduce-window.6
  10.3 0.2 slice_reduce_fusion
  10.6 0.1 fusion.17
  10.7 4.8 %scatter_custom_fusion = bf16[1024,1024]{1,0:T(8,128)(2,1)} fusion(s32[512]{0:T(512)S(1)} %bitcast.43, bf16[64,8,1024]{2,1,0:T(8,128)(2,1)} %param.4, bf16[]{:T(256)} %constant.6.clone.1), kind=kCustom, calls=%fused_computation.10 | custom fusion | bytes 3145730 | tf_op jit(solution)/shard_map/scatter | solution.py:25
  15.4 8.4 %all-to-all-start = ((bf16[16,64,1024]{2,1,0:T(8,128)(2,1)}), bf16[16,64,1024]{2,1,0:T(8,128)(2,1)}, u32[]{:S(2)}, u32[]{:S(2)}) async-start(bf16[16,64,1024]{2,1,0:T(8,128)(2,1)} %bitcast.41), calls=%async_computation | async-start | bytes 4194304 | tf_op jit(solution)/shard_map/all_to_all | solution.py:27
  23.9 5.2 %fusion.4 = f32[1024,256]{1,0:T(8,128)S(1)} fusion(bf16[3584,256]{1,0:T(8,128)(2,1)S(1)} %copy-done, bf16[1,3584,1024]{2,1,0:T(8,128)(2,1)} %param.6), kind=kOutput, calls=%fused_computation.5 | convolution fusion | flops 1879048192 | bytes 10223616 | tf_op jit(solution)/shard_map/dot_general | solution.py:14
  29.0 6.3 %all-reduce.4 = bf16[1024,256]{1,0:T(8,128)(2,1)S(1)} all-reduce(f32[1024,256]{1,0:T(8,128)S(1)} %fusion.4), channel_id=1, replica_groups=mesh['expert'=16,'seq'=2] {'seq'}, use_global_device_ids=true, to_apply=%region_4.5 | all-reduce | flops 262144 | bytes 1572864 | tf_op jit(solution)/shard_map/psum | solution.py:17
  35.3 31.6 %all-to-all-done = bf16[16,64,1024]{2,1,0:T(8,128)(2,1)} async-done(((bf16[16,64,1024]{2,1,0:T(8,128)(2,1)}), bf16[16,64,1024]{2,1,0:T(8,128)(2,1)}, u32[]{:S(2)}, u32[]{:S(2)}) %all-to-all-start) | async-done | bytes 2097184 | tf_op jit(solution)/shard_map/all_to_all | solution.py:27
  66.9 5.4 %fusion.9 = f32[1024,256]{1,0:T(8,128)} fusion(bf16[1024,1024]{1,0:T(8,128)(2,1)} %bitcast.5, bf16[1024,256]{1,0:T(8,128)(2,1)S(1)} %all-reduce.4), kind=kOutput, calls=%fused_computation.9 | convolution fusion | flops 1074003968 | bytes 3670016 | tf_op jit(solution)/shard_map/dot_general | solution.py:32
  72.4 24.1 %all-reduce.3.cloned.1.call-done = f32[1024,256]{1,0:T(8,128)} async-done(((f32[1024,256]{1,0:T(8,128)}), f32[1024,256]{1,0:T(8,128)}) %all-reduce.3.cloned.1.call-update) | async-done | bytes 1048592 | tf_op jit(solution)/shard_map/psum | solution.py:35
  96.5 7.3 %fusion.6 = f32[3584,256]{0,1:T(8,128)} fusion(bf16[1,3584,1024]{2,1,0:T(8,128)(2,1)} %param.6, f32[1024,256]{1,0:T(8,128)} %all-reduce.3.cloned.1.call-done), kind=kOutput, calls=%fused_computation.7 | convolution fusion | flops 1879572480 | bytes 12058624 | tf_op jit(solution)/shard_map/dot_general | solution.py:36
  103.8 5.1 %copy.24 = f32[3584,256]{1,0:T(8,128)} copy(f32[3584,256]{0,1:T(8,128)} %fusion.6) | data formatting | bytes 7340032
  109.0 0.0 all-gather.2.cloned.1.call-start
  109.1 87.1 %reduce-scatter.7.cloned.1.call-done = f32[224,256]{1,0:T(8,128)} async-done(((f32[3584,256]{1,0:T(8,128)}), f32[224,256]{1,0:T(8,128)}) %reduce-scatter.7.cloned.1.call-update) | async-done | bytes 229392
  196.2 1.6 convert_element_type.21
  197.9 59.7 %all-gather.2.cloned.1.call-done = bf16[3584,256]{1,0:T(8,128)(2,1)} async-done(((bf16[224,256]{1,0:T(8,128)(2,1)}), bf16[3584,256]{1,0:T(8,128)(2,1)}) %all-gather.2.cloned.1.call-update) | async-done | bytes 1835024 | tf_op jit(solution)/shard_map/all_gather | solution.py:41
  257.5 6.7 %fusion = f32[256,1024]{1,0:T(8,128)} fusion(bf16[3584,256]{1,0:T(8,128)(2,1)} %all-gather.2.cloned.1.call-done, bf16[1,3584,1024]{2,1,0:T(8,128)(2,1)} %param.6), kind=kOutput, calls=%fused_computation.1 | convolution fusion | flops 1879048192 | bytes 10223616 | tf_op jit(solution)/shard_map/dot_general | solution.py:40
  264.3 7.5 %reduce-scatter.5.cloned.1.call-done = f32[256,512]{1,0:T(8,128)} async-done(((f32[256,1024]{1,0:T(8,128)}), f32[256,512]{1,0:T(8,128)}) %reduce-scatter.5.cloned.1.call-update) | async-done | bytes 524304 | tf_op jit(solution)/shard_map/reduce_scatter | solution.py:46
  (13 shorter events, 0.3 us)
Async XLA Ops:
  7.2 16.7 %copy-start = (bf16[3584,256]{1,0:T(8,128)(2,1)S(1)}, bf16[3584,256]{1,0:T(8,128)(2,1)}, u32[]{:S(2)}) copy-start(bf16[3584,256]{1,0:T(8,128)(2,1)} %param.7) | copy-start | bytes 5505028
  15.4 51.5 %all-to-all-start = ((bf16[16,64,1024]{2,1,0:T(8,128)(2,1)}), bf16[16,64,1024]{2,1,0:T(8,128)(2,1)}, u32[]{:S(2)}, u32[]{:S(2)}) async-start(bf16[16,64,1024]{2,1,0:T(8,128)(2,1)} %bitcast.41), calls=%async_computation | async-start | bytes 4194304 | tf_op jit(solution)/shard_map/all_to_all | solution.py:27
  23.8 72.7 %all-reduce.3.cloned.1.call-start = ((), (), s32[]{:S(2)}) async-start(), calls=%async_computation.3 | async-start | bytes 2097152 | tf_op jit(solution)/shard_map/psum | solution.py:35
  72.4 123.8 %reduce-scatter.7.cloned.1.call-start = ((), (), s32[]{:S(2)}) async-start(), calls=%async_computation.6 | async-start | bytes 3899392
  109.0 148.5 %all-gather.2.cloned.1.call-start = ((), (), s32[]{:S(2)}) async-start(), calls=%async_computation.4 | async-start | bytes 1949696 | tf_op jit(solution)/shard_map/all_gather | solution.py:41
  197.8 74.0 %reduce-scatter.5.cloned.1.call-start = ((), (), s32[]{:S(2)}) async-start(), calls=%async_computation.5 | async-start | bytes 1572864 | tf_op jit(solution)/shard_map/reduce_scatter | solution.py:46
Sparse Core Ops, SparseCore 0:
  72.5 23.9 all-reduce.2
  109.1 87.0 reduce-scatter.6
  199.8 57.6 all-gather.1
  264.4 7.3 reduce-scatter.4
where the time goes:
time: 279 us; the launch traced here: 278 us
  waiting for transfers between devices  210 us (75%)
  matrix products  24.7 us (9%)
  between operations  13.8 us (5%)
  local copies, waits for them, and re-layouts  11.3 us (4%)
  starting transfers between devices  8.53 us (3%)
  blocking collectives  6.27 us (2%)
  other arithmetic  3.72 us (1%)
    unnamed x5, waiting for transfers between devices  87.2 us
    all_gather x1, waiting for transfers between devices, body(): lax.all_gather(basis_rows.astype(jnp.bfloat16), 'expert', axis=0, tiled=T...  59.7 us
    all_to_all x1, waiting for transfers between devices, body(): lax.all_to_all(outgoing, 'expert', split_axis=0, concat_axis=0, tiled=True)  31.6 us
    psum x1, waiting for transfers between devices, body(): gram_full = lax.psum(gram_part, 'seq') / row_mean  24.1 us
    all_to_all x1, starting transfers between devices, body(): lax.all_to_all(outgoing, 'expert', split_axis=0, concat_axis=0, tiled=True)  8.36 us
    reduce_scatter x1, waiting for transfers between devices, body(): lax.psum_scatter(coef_part, 'seq', scatter_dimension=1, tiled=True)  7.53 us
    dot_general x1, matrix products, body(): jnp.dot(weight, gram_full.astype(jnp.bfloat16), preferred_element_type=jn...  7.34 us
    dot_general x1, matrix products, body(): lax.dot_general(lax.all_gather(basis_rows.astype(jnp.bfloat16), 'expert',...  6.72 us
  transfers between devices with their start and end apart: 5, of which 5 were waited for; matrix products, arithmetic and copies ran while one was open for 2% of the time, Pallas kernels for 0%

commit v1 on v0

--- a/solution.py
+++ b/solution.py
@@ -1,7 +1,285 @@
+import functools
+
 import jax
 import jax.numpy as jnp
 from jax import lax
+from jax.experimental import pallas as pl
+from jax.experimental.pallas import tpu as pltpu
 from jax.sharding import PartitionSpec as P
+
+MESH = pl.DeviceIdType.MESH
+F32 = jnp.float32
+BF16 = jnp.bfloat16
+
+
+def contract0(a, b):
+    return lax.dot_general(a, b, (((0,), (0,)), ((), ())), preferred_element_type=F32)
+
+
+def panel_kernel(
+    row_mean, w, gram, basis_out, coef_out,
+    g_recv, g_bf, sa1, sb1, ra1, rb1, pa2, pb2, p3, sa2, sb2, ra2, rb2, s3, r3, gath, coef, c_recv,
+    g_sem, a1_sem, b1_sem, a2_sem, b2_sem, z_sem, gz_sem, ga1_sem, gb1_sem, ga2_sem, gb2_sem, c_sem,
+):
+    e, s = lax.axis_index("expert"), lax.axis_index("seq")
+    x, y, z = e % 2, (e // 2) % 2, e // 4
+    to_x = {"expert": e + 1 - 2 * x}
+    to_y = {"expert": e + 2 - 4 * y}
+    to_core = {"seq": 1 - s}
+    to_z = lambda d: {"expert": ((z + d) % 4) * 4 + e % 4}
+    rows, half = basis_out.shape[0], basis_out.shape[1] // 2
+
+    def chunk(zz, yr, xr):
+        return zz * 4 + ((y + yr) % 2) * 2 + (x + xr) % 2
+
+    def w_rows(c):
+        return w[pl.ds(pl.multiple_of(c * rows, rows), rows), :]
+
+    def remote(src, dst, sem, at, where):
+        return pltpu.make_async_remote_copy(
+            src_ref=src, dst_ref=dst, send_sem=sem.at[(0, *at)], recv_sem=sem.at[(1, *at)],
+            device_id=where, device_id_type=MESH,
+        )
+
+    barrier = pltpu.get_barrier_semaphore()
+    for where in (to_x, to_y, to_core, to_z(1), to_z(2), to_z(3)):
+        pl.semaphore_signal(barrier, inc=1, device_id=where, device_id_type=MESH)
+    pl.semaphore_wait(barrier, 6)
+
+    swap = remote(gram, g_recv, g_sem, (), to_core)
+    swap.start()
+    swap.wait()
+    g_bf[...] = ((gram[...] + g_recv[...]) / row_mean).astype(BF16)
+
+    def panel(d, yr, xr):
+        return jnp.dot(w_rows(chunk((z + d) % 4, yr, xr)), g_bf[...], preferred_element_type=F32)
+
+    copy_a1 = lambda yr, d: remote(sa1.at[yr, d], ra1.at[yr, d], a1_sem, (yr, d), to_x)
+    copy_b1 = lambda xr, d: remote(sb1.at[xr, d], rb1.at[xr, d], b1_sem, (xr, d), to_y)
+    copy_a2 = lambda d: remote(sa2.at[d], ra2.at[d], a2_sem, (d,), to_y)
+    copy_b2 = lambda d: remote(sb2.at[d], rb2.at[d], b2_sem, (d,), to_x)
+    copy_z = lambda d: remote(s3.at[d], r3.at[d], z_sem, (d,), to_z(d))
+
+    def over_z(step):
+        lax.fori_loop(0, 4, lambda i, carry: (step((i + 1) % 4), carry)[1], 0)
+
+    def both_far(d):
+        value = panel(d, 1, 1)
+        sa1[1, d] = value[:, :half].astype(BF16)
+        copy_a1(1, d).start()
+        sb1[1, d] = value[:, half:].astype(BF16)
+        copy_b1(1, d).start()
+
+    def one_far(d):
+        value = panel(d, 0, 1)
+        sa1[0, d] = value[:, :half].astype(BF16)
+        copy_a1(0, d).start()
+        pb2[d] = value[:, half:]
+        value = panel(d, 1, 0)
+        sb1[0, d] = value[:, half:].astype(BF16)
+        copy_b1(0, d).start()
+        pa2[d] = value[:, :half]
+
+    def near(d):
+        p3[d] = panel(d, 0, 0)
+
+    def second(d):
+        copy_a1(1, d).wait_recv()
+        sa2[d] = (pa2[d] + ra1[1, d].astype(F32)).astype(BF16)
+        copy_a2(d).start()
+        copy_b1(1, d).wait_recv()
+        sb2[d] = (pb2[d] + rb1[1, d].astype(F32)).astype(BF16)
+        copy_b2(d).start()
+
+    def third(d):
+        copy_a1(0, d).wait_recv()
+        copy_a2(d).wait_recv()
+        first = p3[d, :, :half] + ra1[0, d].astype(F32) + ra2[d].astype(F32)
+        copy_b1(0, d).wait_recv()
+        copy_b2(d).wait_recv()
+        last = p3[d, :, half:] + rb1[0, d].astype(F32) + rb2[d].astype(F32)
+        return first, last
+
+    def third_send(i, carry):
+        d = i + 1
+        first, last = third(d)
+        s3[d, 0] = first.astype(BF16)
+        s3[d, 1] = last.astype(BF16)
+        copy_z(d).start()
+        return carry
+
+    over_z(both_far)
+    over_z(one_far)
+    over_z(near)
+    over_z(second)
+    lax.fori_loop(0, 3, third_send, 0)
+    first, last = third(0)
+    for d in (1, 2, 3):
+        copy_z(d).wait_recv()
+        first += r3[d, 0].astype(F32)
+        last += r3[d, 1].astype(F32)
+    basis_out[:, :half] = first
+    basis_out[:, half:] = last
+    gath[e, 0] = first.astype(BF16)
+    gath[e, 1] = last.astype(BF16)
+
+    def held(d, yr, xr):
+        return chunk((z + 4 - d) % 4, yr, xr)
+
+    def pass_on(c, part, sem, at, where):
+        return remote(gath.at[c, part], gath.at[c, part], sem, at, where)
+
+    copy_gz = lambda d: remote(gath.at[e], gath.at[e], gz_sem, (d,), to_z(d))
+    copy_ga1 = lambda d: pass_on(held(d, 0, 0), 0, ga1_sem, (d,), to_y)
+    copy_gb1 = lambda d: pass_on(held(d, 0, 0), 1, gb1_sem, (d,), to_x)
+    copy_ga2 = lambda yr, d: pass_on(held(d, yr, 0), 0, ga2_sem, (yr, d), to_x)
+    copy_gb2 = lambda xr, d: pass_on(held(d, 0, xr), 1, gb2_sem, (xr, d), to_y)
+
+    def came_z(d):
+        c = held(d, 0, 0)
+        return remote(gath.at[c], gath.at[c], gz_sem, (d,), to_z(d))
+
+    def came_a1(d):
+        return pass_on(held(d, 1, 0), 0, ga1_sem, (d,), to_y)
+
+    def came_b1(d):
+        return pass_on(held(d, 0, 1), 1, gb1_sem, (d,), to_x)
+
+    def came_a2(yr, d):
+        return pass_on(held(d, yr, 1), 0, ga2_sem, (yr, d), to_x)
+
+    def came_b2(xr, d):
+        return pass_on(held(d, 1, xr), 1, gb2_sem, (xr, d), to_y)
+
+    for d in (2, 1, 3):
+        copy_gz(d).start()
+    coef[...] = jnp.zeros_like(coef)
+
+    def add_coef(c):
+        block = jnp.concatenate([gath[c, 0], gath[c, 1]], axis=1)
+        value = contract0(block, w_rows(c))
+        width = value.shape[1] // 2
+        coef[0] += value[:, :width]
+        coef[1] += value[:, width:]
+
+    def hand_out(d):
+        copy_ga1(d).start()
+        copy_gb1(d).start()
+        copy_ga2(0, d).start()
+        copy_gb2(0, d).start()
+
+    hand_out(0)
+
+    def from_z(i, carry):
+        came_z(i + 1).wait_recv()
+        hand_out(i + 1)
+        return carry
+
+    lax.fori_loop(0, 3, from_z, 0)
+
+    def forward(d, carry):
+        came_a1(d).wait_recv()
+        copy_ga2(1, d).start()
+        came_b1(d).wait_recv()
+        copy_gb2(1, d).start()
+        add_coef(held(d, 0, 0))
+        return carry
+
+    lax.fori_loop(0, 4, forward, 0)
+
+    def take_near(d, carry):
+        came_b2(0, d).wait_recv()
+        add_coef(held(d, 1, 0))
+        came_a2(0, d).wait_recv()
+        add_coef(held(d, 0, 1))
+        return carry
+
+    lax.fori_loop(0, 4, take_near, 0)
+
+    def take_far(d, carry):
+        came_a2(1, d).wait_recv()
+        came_b2(1, d).wait_recv()
+        add_coef(held(d, 1, 1))
+        return carry
+
+    lax.fori_loop(0, 4, take_far, 0)
+
+    share = remote(coef.at[1 - s], c_recv, c_sem, (), to_core)
+    share.start()
+
+    def drain(d, carry):
+        for k in (0, 1):
+            copy_a1(k, d).wait_send()
+            copy_b1(k, d).wait_send()
+            copy_ga2(k, d).wait_send()
+            copy_gb2(k, d).wait_send()
+        copy_a2(d).wait_send()
+        copy_b2(d).wait_send()
+        copy_ga1(d).wait_send()
+        copy_gb1(d).wait_send()
+        return carry
+
+    lax.fori_loop(0, 4, drain, 0)
+    for d in (1, 2, 3):
+        copy_z(d).wait_send()
+        copy_gz(d).wait_send()
+    share.wait()
+    coef_out[...] = coef[s] + c_recv[...]
+
+
+def panel_call(weight, gram_part, row_mean):
+    depth, width = weight.shape
+    cols = gram_part.shape[1]
+    rows, half = depth // 16, cols // 2
+    dma = pltpu.SemaphoreType.DMA
+    vmem = pltpu.VMEM
+    return pl.pallas_call(
+        functools.partial(panel_kernel, row_mean),
+        out_shape=(
+            jax.ShapeDtypeStruct((rows, cols), F32),
+            jax.ShapeDtypeStruct((cols, width // 2), F32),
+        ),
+        in_specs=[pl.BlockSpec(memory_space=vmem)] * 2,
+        out_specs=[pl.BlockSpec(memory_space=vmem)] * 2,
+        scratch_shapes=[
+            vmem((width, cols), F32),
+            vmem((width, cols), BF16),
+            vmem((2, 4, rows, half), BF16),
+            vmem((2, 4, rows, half), BF16),
+            vmem((2, 4, rows, half), BF16),
+            vmem((2, 4, rows, half), BF16),
+            vmem((4, rows, half), F32),
+            vmem((4, rows, half), F32),
+            vmem((4, rows, cols), F32),
+            vmem((4, rows, half), BF16),
+            vmem((4, rows, half), BF16),
+            vmem((4, rows, half), BF16),
+            vmem((4, rows, half), BF16),
+            vmem((4, 2, rows, half), BF16),
+            vmem((4, 2, rows, half), BF16),
+            vmem((16, 2, rows, half), BF16),
+            vmem((2, cols, width // 2), F32),
+            vmem((cols, width // 2), F32),
+            dma((2,)),
+            dma((2, 2, 4)),
+            dma((2, 2, 4)),
+            dma((2, 4)),
+            dma((2, 4)),
+            dma((2, 4)),
+            dma((2, 4)),
+            dma((2, 4)),
+            dma((2, 4)),
+            dma((2, 2, 4)),
+            dma((2, 2, 4)),
+            dma((2,)),
+        ],
+        compiler_params=pltpu.CompilerParams(
+            collective_id=0, has_side_effects=True, vmem_limit_bytes=40 * 2**20
+        ),
+        cost_estimate=pl.CostEstimate(
+            flops=4 * depth * width * cols, bytes_accessed=2 * depth * width, transcendentals=0
+        ),
+    )(weight, gram_part)
 
 
 def body(hidden_rows, routes, down_weight, probe):
@@ -32,6 +310,9 @@
     gram_part = lax.dot_general(
         arrived_rows, mixed, (((0,), (0,)), ((), ())), preferred_element_type=jnp.float32
     )
+    if experts == 16 and lax.axis_size("seq") == 2:
+        basis_rows, coefficients = panel_call(weight, gram_part, row_mean)
+        return (basis_rows, coefficients[None])
     gram_full = lax.psum(gram_part, "seq") / row_mean
     panel_image = jnp.dot(
         weight, gram_full.astype(jnp.bfloat16), preferred_element_type=jnp.float32

time: 279 us -> 131 us (0.47)
  waiting for transfers between devices: 210 us -> 31.6 us
  Pallas kernels: 0 us -> 59.5 us
  matrix products: 24.7 us -> 9.63 us
  between operations: 13.8 us -> 0.7 us
    unnamed x5 -> x0, waiting for transfers between devices: 87.2 us -> none
    all_gather x1 -> x0, waiting for transfers between devices: 59.7 us -> none  [body(): lax.all_gather(basis_rows.astype(jnp.bfloat16), 'expert', axis=0, tiled=T...]
    pallas_call x0 -> x1, Pallas kernels: none -> 59.5 us  [panel_call(): pl.pallas_call(functools.partial(panel_kernel, row_mean), out_shape=(jax....]
    psum x1 -> x0, waiting for transfers between devices: 24.1 us -> none  [body(): gram_full = lax.psum(gram_part, 'seq') / row_mean]
    dot_general x2 -> x0, matrix products: 14.1 us -> none  [the longest x1 7.34 us: body(): jnp.dot(weight, gram_full.astype(jnp.bfloat16), preferred_element_type=jn...]
    reduce_scatter x1 -> x0, waiting for transfers between devices: 7.53 us -> none  [body(): lax.psum_scatter(coef_part, 'seq', scatter_dimension=1, tiled=True)]
    unnamed x4 -> x7, local copies, waits for them, and re-layouts: 5.93 us -> 5.5 us
  transfers between devices with their start and end apart: 5 -> 1, of which waited for: 5 -> 1; matrix products, arithmetic and copies ran while one was open for 2% -> 4% of each run, Pallas kernels for 0% -> 0%
where the time goes in v1:
time: 131 us; the launch traced here: 129 us
  Pallas kernels  59.5 us (45%)
  waiting for transfers between devices  31.6 us (24%)
  local copies, waits for them, and re-layouts  10.8 us (8%)
  matrix products  9.63 us (7%)
  starting transfers between devices  8.36 us (6%)
  blocking collectives  6.27 us (5%)
  other arithmetic  1.98 us (2%)
    pallas_call x1, Pallas kernels, panel_call(): pl.pallas_call(functools.partial(panel_kernel, row_mean), out_shape=(jax....  59.5 us
    all_to_all x1, waiting for transfers between devices, body(): lax.all_to_all(outgoing, 'expert', split_axis=0, concat_axis=0, tiled=True)  31.6 us
    all_to_all x1, starting transfers between devices, body(): lax.all_to_all(outgoing, 'expert', split_axis=0, concat_axis=0, tiled=True)  8.36 us
    psum x1, blocking collectives, body(): probe_proj = lax.psum(partial_value, 'seq').astype(jnp.bfloat16)  6.27 us
    unnamed x7, local copies, waits for them, and re-layouts  5.5 us
    dot_general x1, matrix products, body(): lax.dot_general(weight, probe, (((0,), (0,)), ((), ())), preferred_elemen...  5.19 us
    scatter x1, local copies, waits for them, and re-layouts, body(): outgoing.at[destination].set(hidden_rows.reshape(-1, feature_width))  4.77 us
    dot_general x1, matrix products, body(): lax.dot_general(arrived_rows, mixed, (((0,), (0,)), ((), ())), preferred_...  4.44 us
  transfers between devices with their start and end apart: 1, of which 1 were waited for; matrix products, arithmetic and copies ran while one was open for 4% of the time, Pallas kernels for 0%

profile of v1, /device:TPU:0, one launch (start us, length us, event | category | flops | bytes accessed | tf_op | source)
XLA Modules:
  0.0 128.9 jit_solution(11219891677902255549)
XLA Ops:
  0.6 0.0 copy-start
  0.6 0.9 copy.7
  1.6 0.1 eq.29
  1.6 0.1 eq.25
  1.7 0.7 broadcast_multiply_fusion
  2.4 1.1 reduce-window.6
  3.6 0.2 slice_reduce_fusion
  3.8 0.1 copy.6
  3.9 0.1 mul.21
  4.0 0.1 fusion.7
  4.1 4.8 %scatter_custom_fusion = bf16[1024,1024]{1,0:T(8,128)(2,1)} fusion(s32[512]{0:T(512)S(1)} %bitcast.34, bf16[64,8,1024]{2,1,0:T(8,128)(2,1)} %param.4, bf16[]{:T(256)} %constant.5.clone.1), kind=kCustom, calls=%fused_computation.3 | custom fusion | bytes 3145730 | tf_op jit(solution)/shard_map/scatter | solution.py:303
  8.9 8.4 %all-to-all-start = ((bf16[16,64,1024]{2,1,0:T(8,128)(2,1)}), bf16[16,64,1024]{2,1,0:T(8,128)(2,1)}, u32[]{:S(2)}, u32[]{:S(2)}) async-start(bf16[16,64,1024]{2,1,0:T(8,128)(2,1)} %bitcast.32), calls=%async_computation | async-start | bytes 4194304 | tf_op jit(solution)/shard_map/all_to_all | solution.py:305
  17.3 0.0 copy-done
  17.3 5.2 %fusion.9 = f32[1024,256]{1,0:T(8,128)S(1)} fusion(bf16[3584,256]{1,0:T(8,128)(2,1)S(1)} %copy-done, bf16[1,3584,1024]{2,1,0:T(8,128)(2,1)} %param.6), kind=kOutput, calls=%fused_computation.17 | convolution fusion | flops 1879048192 | bytes 10223616 | tf_op jit(solution)/shard_map/dot_general | solution.py:292
  22.5 6.3 %all-reduce.1 = bf16[1024,256]{1,0:T(8,128)(2,1)S(1)} all-reduce(f32[1024,256]{1,0:T(8,128)S(1)} %fusion.9), channel_id=1, replica_groups=mesh['expert'=16,'seq'=2] {'seq'}, use_global_device_ids=true, to_apply=%region_4.5 | all-reduce | flops 262144 | bytes 1572864 | tf_op jit(solution)/shard_map/psum | solution.py:295
  28.8 31.6 %all-to-all-done = bf16[16,64,1024]{2,1,0:T(8,128)(2,1)} async-done(((bf16[16,64,1024]{2,1,0:T(8,128)(2,1)}), bf16[16,64,1024]{2,1,0:T(8,128)(2,1)}, u32[]{:S(2)}, u32[]{:S(2)}) %all-to-all-start) | async-done | bytes 2097184 | tf_op jit(solution)/shard_map/all_to_all | solution.py:305
  60.4 4.4 %fusion.gram = f32[1024,256]{1,0:T(8,128)S(1)} fusion(bf16[1024,1024]{1,0:T(8,128)(2,1)} %bitcast.6, bf16[1024,256]{1,0:T(8,128)(2,1)S(1)} %all-reduce.1), kind=kOutput, calls=%fused_computation.2 | convolution fusion | flops 1074003968 | bytes 3670016 | tf_op jit(solution)/shard_map/dot_general | solution.py:310
  64.8 0.0 copy-start.1
  64.8 3.1 %copy-done.1 = bf16[1,3584,1024]{2,1,0:T(8,128)(2,1)S(1)} copy-done((bf16[1,3584,1024]{2,1,0:T(8,128)(2,1)S(1)}, bf16[1,3584,1024]{2,1,0:T(8,128)(2,1)}, u32[]{:S(2)}) %copy-start.1) | copy-done | bytes 7340056
  67.9 59.5 %shard_map.59 = (f32[224,256]{1,0:T(8,128)S(1)}, f32[256,512]{1,0:T(8,128)S(1)}) custom-call(bf16[3584,1024]{1,0:T(8,128)(2,1)S(1)} %bitcast.30, f32[1024,256]{1,0:T(8,128)S(1)} %fusion.gram), custom_call_target="tpu_custom_call" | custom-call | flops 3758096384 | bytes 7340032 | tf_op jit(solution)/shard_map/pallas_call | solution.py:236
  127.4 0.7 copy.16
  128.1 0.8 copy.17
  (4 shorter events, 0.1 us)
Async XLA Ops:
  0.6 16.6 %copy-start = (bf16[3584,256]{1,0:T(8,128)(2,1)S(1)}, bf16[3584,256]{1,0:T(8,128)(2,1)}, u32[]{:S(2)}) copy-start(bf16[3584,256]{1,0:T(8,128)(2,1)} %param.7) | copy-start | bytes 5505028
  8.9 51.5 %all-to-all-start = ((bf16[16,64,1024]{2,1,0:T(8,128)(2,1)}), bf16[16,64,1024]{2,1,0:T(8,128)(2,1)}, u32[]{:S(2)}, u32[]{:S(2)}) async-start(bf16[16,64,1024]{2,1,0:T(8,128)(2,1)} %bitcast.32), calls=%async_computation | async-start | bytes 4194304 | tf_op jit(solution)/shard_map/all_to_all | solution.py:305
  64.8 3.1 %copy-start.1 = (bf16[1,3584,1024]{2,1,0:T(8,128)(2,1)S(1)}, bf16[1,3584,1024]{2,1,0:T(8,128)(2,1)}, u32[]{:S(2)}) copy-start(bf16[1,3584,1024]{2,1,0:T(8,128)(2,1)} %param.6) | copy-start | bytes 22020100

commit v2 on v1

--- a/solution.py
+++ b/solution.py
@@ -16,10 +16,14 @@
     return lax.dot_general(a, b, (((0,), (0,)), ((), ())), preferred_element_type=F32)
 
 
+def contract1(a, b):
+    return lax.dot_general(a, b, (((1,), (1,)), ((), ())), preferred_element_type=F32)
+
+
 def panel_kernel(
-    row_mean, w, gram, basis_out, coef_out,
-    g_recv, g_bf, sa1, sb1, ra1, rb1, pa2, pb2, p3, sa2, sb2, ra2, rb2, s3, r3, gath, coef, c_recv,
-    g_sem, a1_sem, b1_sem, a2_sem, b2_sem, z_sem, gz_sem, ga1_sem, gb1_sem, ga2_sem, gb2_sem, c_sem,
+    row_mean, w_any, probe_any, ids, tokens, basis_out, coef_out,
+    w, probe, sent, arr, p_part, p_recv, pt, gt, gr, sp, rp, g_bf, sa1, sb1, ra1, rb1, pa2, pb2, p3, sa2, sb2, ra2, rb2, s3, r3, gath, coef, c_recv,
+    load_sem, rows_sem, p_sem, px_sem, pf_sem, gs_sem, gx_sem, gf_sem, a1_sem, b1_sem, a2_sem, b2_sem, z_sem, gz_sem, ga1_sem, gb1_sem, ga2_sem, gb2_sem, c_sem,
 ):
     e, s = lax.axis_index("expert"), lax.axis_index("seq")
     x, y, z = e % 2, (e // 2) % 2, e // 4
@@ -41,18 +45,121 @@
             device_id=where, device_id_type=MESH,
         )
 
+    cap = tokens.shape[0] // 8
+    own_half = z // 2
+    partner = {"expert": (e + 8) % 16}
+
+    def near_chip(q):
+        return own_half * 8 + (z + q // 4) % 2 * 4 + (y + q // 2) % 2 * 2 + (x + q) % 2
+
+    load_w = pltpu.make_async_copy(w_any, w, load_sem.at[0])
+    load_probe = pltpu.make_async_copy(probe_any, probe, load_sem.at[1])
+    load_w.start()
+    load_probe.start()
+
     barrier = pltpu.get_barrier_semaphore()
-    for where in (to_x, to_y, to_core, to_z(1), to_z(2), to_z(3)):
+    for q in range(1, 8):
+        pl.semaphore_signal(
+            barrier, inc=1, device_id={"expert": near_chip(q)}, device_id_type=MESH
+        )
+    far = [{"expert": (2 - 2 * own_half + k) * 4 + e % 4} for k in (0, 1)]
+    for where in (to_core, *far):
         pl.semaphore_signal(barrier, inc=1, device_id=where, device_id_type=MESH)
-    pl.semaphore_wait(barrier, 6)
-
-    swap = remote(gram, g_recv, g_sem, (), to_core)
+
+    amount = tokens.shape[0]
+    names = ids[...]
+    mark = (lax.broadcasted_iota(jnp.int32, (16, amount), 0) == names).astype(F32)
+    before = (
+        lax.broadcasted_iota(jnp.int32, (amount, amount), 0)
+        < lax.broadcasted_iota(jnp.int32, (amount, amount), 1)
+    ).astype(F32).astype(BF16)
+    rank = jnp.dot(mark.astype(BF16), before, preferred_element_type=F32)
+    place = jnp.sum(mark * rank, axis=0, keepdims=True).astype(jnp.int32) + names * cap
+
+    copy_rows = lambda k, q: remote(
+        sent.at[k, q], arr.at[k, q], rows_sem, (k, q), {"expert": near_chip(q)}
+    )
+
+    def block_for(q):
+        chip = near_chip(q)
+        line = lax.broadcasted_iota(jnp.int32, (2 * cap, amount), 0)
+        wanted = jnp.where(line < cap, chip * cap + line, ((chip + 8) % 16 - 1) * cap + line)
+        pick = (wanted == place).astype(F32).astype(BF16)
+        return jnp.dot(pick, tokens[...], preferred_element_type=F32).astype(BF16)
+
+    pl.semaphore_wait(barrier, 10)
+
+    def send_rows(i, carry):
+        q = 7 - i
+        block = block_for(q)
+        sent[0, q] = block[:cap]
+        copy_rows(0, q).start()
+        sent[1, q] = block[cap:]
+        copy_rows(1, q).start()
+        return carry
+
+    lax.fori_loop(0, 7, send_rows, 0)
+    block = block_for(0)
+    arr[0, 0] = block[:cap]
+    arr[1, 0] = block[cap:]
+
+    load_probe.wait()
+    load_w.wait()
+    p_part[...] = jnp.zeros_like(p_part)
+    part = 256
+
+    def project(i, carry):
+        at = pl.ds(pl.multiple_of(i * part, part), part)
+        p_part[...] += contract0(probe[at, :], w[at, :])
+        return carry
+
+    lax.fori_loop(0, w.shape[0] // part, project, 0)
+    swap = remote(p_part, p_recv, p_sem, (), to_core)
     swap.start()
     swap.wait()
-    g_bf[...] = ((gram[...] + g_recv[...]) / row_mean).astype(BF16)
+    pt[0] = (p_part[...] + p_recv[...]).astype(BF16).reshape(pt.shape[1:])
+    across = remote(pt.at[0, s], pt.at[1, s], px_sem, (), partner)
+    across.start()
+
+    def gram_of(k, first):
+        rows_k = arr[k, first:first + 4].reshape(4 * cap, arr.shape[3])
+        proj = pt[k].reshape(2 * pt.shape[2], pt.shape[3])
+        mixed = contract1(rows_k, proj).astype(BF16)
+        return contract0(mixed, rows_k).reshape(gt.shape[1:])
+
+    for q in (3, 2, 1):
+        copy_rows(0, q).wait_recv()
+    gt[0] = gram_of(0, 0)
+    across.wait_recv()
+    hand = remote(pt.at[1, s], pt.at[1, s], pf_sem, (), to_core)
+    hand.start()
+    for q in (3, 2, 1):
+        copy_rows(1, q).wait_recv()
+    remote(pt.at[1, 1 - s], pt.at[1, 1 - s], pf_sem, (), to_core).wait_recv()
+    gt[1] = gram_of(1, 0)
+    for q in (7, 6, 5, 4):
+        copy_rows(1, q).wait_recv()
+    gt[1] += gram_of(1, 4)
+    copy_gs = lambda k: remote(gt.at[k, 1 - s], gr.at[k], gs_sem, (k,), to_core)
+    copy_gs(1).start()
+    for q in (7, 6, 5, 4):
+        copy_rows(0, q).wait_recv()
+    gt[0] += gram_of(0, 4)
+    copy_gs(0).start()
+    copy_gs(1).wait_recv()
+    sp[...] = (gt[1, s] + gr[1]).astype(BF16)
+    cross = remote(sp, rp, gx_sem, (), partner)
+    cross.start()
+    copy_gs(0).wait_recv()
+    cross.wait_recv()
+    g_bf[s] = ((gt[0, s] + gr[0] + rp[...].astype(F32)) / row_mean).astype(BF16)
+    spread = remote(g_bf.at[s], g_bf.at[s], gf_sem, (), to_core)
+    spread.start()
+    remote(g_bf.at[1 - s], g_bf.at[1 - s], gf_sem, (), to_core).wait_recv()
 
     def panel(d, yr, xr):
-        return jnp.dot(w_rows(chunk((z + d) % 4, yr, xr)), g_bf[...], preferred_element_type=F32)
+        g_all = g_bf[...].reshape(2 * half, g_bf.shape[2])
+        return contract1(w_rows(chunk((z + d) % 4, yr, xr)), g_all)
 
     copy_a1 = lambda yr, d: remote(sa1.at[yr, d], ra1.at[yr, d], a1_sem, (yr, d), to_x)
     copy_b1 = lambda xr, d: remote(sb1.at[xr, d], rb1.at[xr, d], b1_sem, (xr, d), to_y)
@@ -170,22 +277,21 @@
 
     hand_out(0)
 
-    def from_z(i, carry):
-        came_z(i + 1).wait_recv()
-        hand_out(i + 1)
-        return carry
-
-    lax.fori_loop(0, 3, from_z, 0)
-
-    def forward(d, carry):
+    def forward(d):
         came_a1(d).wait_recv()
         copy_ga2(1, d).start()
         came_b1(d).wait_recv()
         copy_gb2(1, d).start()
         add_coef(held(d, 0, 0))
-        return carry
-
-    lax.fori_loop(0, 4, forward, 0)
+
+    def from_z(i, carry):
+        came_z(i + 1).wait_recv()
+        hand_out(i + 1)
+        forward(i)
+        return carry
+
+    lax.fori_loop(0, 3, from_z, 0)
+    forward(3)
 
     def take_near(d, carry):
         came_b2(0, d).wait_recv()
@@ -223,13 +329,19 @@
     for d in (1, 2, 3):
         copy_z(d).wait_send()
         copy_gz(d).wait_send()
+    for q in range(1, 8):
+        copy_rows(0, q).wait_send()
+        copy_rows(1, q).wait_send()
+    for copy in (across, hand, copy_gs(0), copy_gs(1), cross, spread):
+        copy.wait_send()
     share.wait()
     coef_out[...] = coef[s] + c_recv[...]
 
 
-def panel_call(weight, gram_part, row_mean):
+def panel_call(weight, probe, ids, tokens, row_mean):
     depth, width = weight.shape
-    cols = gram_part.shape[1]
+    cols = probe.shape[1]
+    cap = tokens.shape[0] // 8
     rows, half = depth // 16, cols // 2
     dma = pltpu.SemaphoreType.DMA
     vmem = pltpu.VMEM
@@ -239,11 +351,21 @@
             jax.ShapeDtypeStruct((rows, cols), F32),
             jax.ShapeDtypeStruct((cols, width // 2), F32),
         ),
-        in_specs=[pl.BlockSpec(memory_space=vmem)] * 2,
+        in_specs=[pl.BlockSpec(memory_space=pl.ANY)] * 2 + [pl.BlockSpec(memory_space=vmem)] * 2,
         out_specs=[pl.BlockSpec(memory_space=vmem)] * 2,
         scratch_shapes=[
-            vmem((width, cols), F32),
-            vmem((width, cols), BF16),
+            vmem((depth, width), BF16),
+            vmem((depth, cols), BF16),
+            vmem((2, 8, cap, width), BF16),
+            vmem((2, 8, cap, width), BF16),
+            vmem((cols, width), F32),
+            vmem((cols, width), F32),
+            vmem((2, 2, half, width), BF16),
+            vmem((2, 2, half, width), F32),
+            vmem((2, half, width), F32),
+            vmem((half, width), BF16),
+            vmem((half, width), BF16),
+            vmem((2, half, width), BF16),
             vmem((2, 4, rows, half), BF16),
             vmem((2, 4, rows, half), BF16),
             vmem((2, 4, rows, half), BF16),
@@ -261,6 +383,13 @@
             vmem((2, cols, width // 2), F32),
             vmem((cols, width // 2), F32),
             dma((2,)),
+            dma((2, 2, 8)),
+            dma((2,)),
+            dma((2,)),
+            dma((2,)),
+            dma((2, 2)),
+            dma((2,)),
+            dma((2,)),
             dma((2, 2, 4)),
             dma((2, 2, 4)),
             dma((2, 4)),
@@ -274,12 +403,12 @@
             dma((2,)),
         ],
         compiler_params=pltpu.CompilerParams(
-            collective_id=0, has_side_effects=True, vmem_limit_bytes=40 * 2**20
+            collective_id=0, has_side_effects=True, vmem_limit_bytes=52 * 2**20
         ),
         cost_estimate=pl.CostEstimate(
-            flops=4 * depth * width * cols, bytes_accessed=2 * depth * width, transcendentals=0
+            flops=8 * depth * width * cols, bytes_accessed=2 * depth * width, transcendentals=0
         ),
-    )(weight, gram_part)
+    )(weight, probe, ids, tokens)
 
 
 def body(hidden_rows, routes, down_weight, probe):
@@ -289,6 +418,11 @@
     experts = lax.axis_size("expert")
     capacity = 2 * tok_count * top_count // experts
     row_mean = tok_count * top_count * lax.axis_size("seq")
+    if experts == 16 and lax.axis_size("seq") == 2:
+        ids = routes.reshape(1, -1)
+        tokens = hidden_rows.reshape(-1, feature_width)
+        basis_rows, coefficients = panel_call(weight, probe, ids, tokens, row_mean)
+        return (basis_rows, coefficients[None])
     partial_value = lax.dot_general(
         weight, probe, (((0,), (0,)), ((), ())), preferred_element_type=jnp.float32
     )
@@ -310,9 +444,6 @@
     gram_part = lax.dot_general(
         arrived_rows, mixed, (((0,), (0,)), ((), ())), preferred_element_type=jnp.float32
     )
-    if experts == 16 and lax.axis_size("seq") == 2:
-        basis_rows, coefficients = panel_call(weight, gram_part, row_mean)
-        return (basis_rows, coefficients[None])
     gram_full = lax.psum(gram_part, "seq") / row_mean
     panel_image = jnp.dot(
         weight, gram_full.astype(jnp.bfloat16), preferred_element_type=jnp.float32

time: 131 us -> 108 us (0.82)
  Pallas kernels: 59.5 us -> 102 us
  waiting for transfers between devices: 31.6 us -> 0 us
  matrix products: 9.63 us -> 0 us
  starting transfers between devices: 8.36 us -> 0 us
  local copies, waits for them, and re-layouts: 10.8 us -> 3.56 us
  blocking collectives: 6.27 us -> 0 us
  other arithmetic: 1.98 us -> 0 us
    pallas_call x1, Pallas kernels: 59.5 us -> 102 us  [panel_call(): pl.pallas_call(functools.partial(panel_kernel, row_mean), out_shape=(jax....]
    all_to_all x1 -> x0, waiting for transfers between devices: 31.6 us -> none  [body(): lax.all_to_all(outgoing, 'expert', split_axis=0, concat_axis=0, tiled=True)]
    dot_general x2 -> x0, matrix products: 9.63 us -> none  [the longest x1 5.19 us: body(): lax.dot_general(weight, probe, (((0,), (0,)), ((), ())), preferred_elemen...]
    all_to_all x1 -> x0, starting transfers between devices: 8.36 us -> none  [body(): lax.all_to_all(outgoing, 'expert', split_axis=0, concat_axis=0, tiled=True)]
    psum x1 -> x0, blocking collectives: 6.27 us -> none  [body(): probe_proj = lax.psum(partial_value, 'seq').astype(jnp.bfloat16)]
    scatter x1 -> x0, local copies, waits for them, and re-layouts: 4.77 us -> none  [body(): outgoing.at[destination].set(hidden_rows.reshape(-1, feature_width))]
    unnamed x7 -> x5, local copies, waits for them, and re-layouts: 5.5 us -> 3.47 us
  transfers between devices with their start and end apart: 1 -> 0, of which waited for: 1 -> 0; matrix products, arithmetic and copies ran while one was open for 4% -> 0% of each run, Pallas kernels for 0% -> 0%
where the time goes in v2:
time: 108 us; the launch traced here: 106 us
  Pallas kernels  102 us (94%)
  local copies, waits for them, and re-layouts  3.56 us (3%)
    pallas_call x1, Pallas kernels, panel_call(): pl.pallas_call(functools.partial(panel_kernel, row_mean), out_shape=(jax....  102 us
    unnamed x5, local copies, waits for them, and re-layouts  3.47 us

profile of v2, /device:TPU:0, one launch (start us, length us, event | category | flops | bytes accessed | tf_op | source)
XLA Modules:
  0.0 106.0 jit_solution(2123467217559644359)
XLA Ops:
  0.6 0.8 copy.7
  1.4 0.1 reshape.10.ids
  1.5 0.0 copy-start
  1.5 1.2 %copy-done = bf16[64,8,1024]{2,1,0:T(8,128)(2,1)S(1)} copy-done((bf16[64,8,1024]{2,1,0:T(8,128)(2,1)S(1)}, bf16[64,8,1024]{2,1,0:T(8,128)(2,1)}, u32[]{:S(2)}) %copy-start) | copy-done | bytes 1048600
  2.7 101.8 %shard_map.59 = (f32[224,256]{1,0:T(8,128)S(1)}, f32[256,512]{1,0:T(8,128)S(1)}) custom-call(bf16[3584,1024]{1,0:T(8,128)(2,1)} %bitcast.5, bf16[3584,256]{1,0:T(8,128)(2,1)} %probe_any.1, s32[1,512]{1,0:T(1,128)S(1)} %reshape.10.ids, bf16[512,1024]{1,0:T(8,128)(2,1)S(1)} %bitcast.4), custom_call_target="tpu_custom_call" | custom-call | flops 7516192768 | bytes 7340032 | tf_op jit(solution)/shard_map/pallas_call | solution.py:348
  104.5 0.7 copy.10
  105.2 0.8 copy.11
Async XLA Ops:
  1.5 1.2 %copy-start = (bf16[64,8,1024]{2,1,0:T(8,128)(2,1)S(1)}, bf16[64,8,1024]{2,1,0:T(8,128)(2,1)}, u32[]{:S(2)}) copy-start(bf16[64,8,1024]{2,1,0:T(8,128)(2,1)} %param.4) | copy-start | bytes 3145732

commit v3 on v2

--- a/solution.py
+++ b/solution.py
@@ -21,8 +21,8 @@
 
 
 def panel_kernel(
-    row_mean, w_any, probe_any, ids, tokens, basis_out, coef_out,
-    w, probe, sent, arr, p_part, p_recv, pt, gt, gr, sp, rp, g_bf, sa1, sb1, ra1, rb1, pa2, pb2, p3, sa2, sb2, ra2, rb2, s3, r3, gath, coef, c_recv,
+    row_mean, w_any, probe_any, tokens_any, ids, basis_out, coef_out,
+    tokens, w, probe, sent, arr, p_part, p_recv, pt, gt, gr, sp, rp, g_bf, sa1, sb1, ra1, rb1, pa2, pb2, p3, sa2, sb2, ra2, rb2, s3, r3, gath, coef, c_recv,
     load_sem, rows_sem, p_sem, px_sem, pf_sem, gs_sem, gx_sem, gf_sem, a1_sem, b1_sem, a2_sem, b2_sem, z_sem, gz_sem, ga1_sem, gb1_sem, ga2_sem, gb2_sem, c_sem,
 ):
     e, s = lax.axis_index("expert"), lax.axis_index("seq")
@@ -30,7 +30,13 @@
     to_x = {"expert": e + 1 - 2 * x}
     to_y = {"expert": e + 2 - 4 * y}
     to_core = {"seq": 1 - s}
-    to_z = lambda d: {"expert": ((z + d) % 4) * 4 + e % 4}
+
+    def z_of(k):
+        return (z // 2 + k // 2) % 2 * 2 + (z + k) % 2
+
+    def to_z(k):
+        return {"expert": z_of(k) * 4 + e % 4}
+
     rows, half = basis_out.shape[0], basis_out.shape[1] // 2
 
     def chunk(zz, yr, xr):
@@ -54,6 +60,8 @@
 
     load_w = pltpu.make_async_copy(w_any, w, load_sem.at[0])
     load_probe = pltpu.make_async_copy(probe_any, probe, load_sem.at[1])
+    load_tokens = pltpu.make_async_copy(tokens_any, tokens, load_sem.at[2])
+    load_tokens.start()
     load_w.start()
     load_probe.start()
 
@@ -76,26 +84,30 @@
     rank = jnp.dot(mark.astype(BF16), before, preferred_element_type=F32)
     place = jnp.sum(mark * rank, axis=0, keepdims=True).astype(jnp.int32) + names * cap
 
-    copy_rows = lambda k, q: remote(
-        sent.at[k, q], arr.at[k, q], rows_sem, (k, q), {"expert": near_chip(q)}
-    )
-
-    def block_for(q):
-        chip = near_chip(q)
+    def slot_chip(i):
+        return near_chip(5 * i % 8)
+
+    copy_rows = lambda k, i: remote(
+        sent.at[k, i], arr.at[k, i], rows_sem, (k, i), {"expert": slot_chip(i)}
+    )
+
+    def block_for(i):
+        chip = slot_chip(i)
         line = lax.broadcasted_iota(jnp.int32, (2 * cap, amount), 0)
         wanted = jnp.where(line < cap, chip * cap + line, ((chip + 8) % 16 - 1) * cap + line)
         pick = (wanted == place).astype(F32).astype(BF16)
         return jnp.dot(pick, tokens[...], preferred_element_type=F32).astype(BF16)
 
+    load_tokens.wait()
     pl.semaphore_wait(barrier, 10)
 
-    def send_rows(i, carry):
-        q = 7 - i
-        block = block_for(q)
-        sent[0, q] = block[:cap]
-        copy_rows(0, q).start()
-        sent[1, q] = block[cap:]
-        copy_rows(1, q).start()
+    def send_rows(j, carry):
+        i = j + 1
+        block = block_for(i)
+        sent[0, i] = block[:cap]
+        copy_rows(0, i).start()
+        sent[1, i] = block[cap:]
+        copy_rows(1, i).start()
         return carry
 
     lax.fori_loop(0, 7, send_rows, 0)
@@ -127,22 +139,22 @@
         mixed = contract1(rows_k, proj).astype(BF16)
         return contract0(mixed, rows_k).reshape(gt.shape[1:])
 
-    for q in (3, 2, 1):
+    for q in (1, 2, 3):
         copy_rows(0, q).wait_recv()
     gt[0] = gram_of(0, 0)
     across.wait_recv()
     hand = remote(pt.at[1, s], pt.at[1, s], pf_sem, (), to_core)
     hand.start()
-    for q in (3, 2, 1):
+    for q in (1, 2, 3):
         copy_rows(1, q).wait_recv()
     remote(pt.at[1, 1 - s], pt.at[1, 1 - s], pf_sem, (), to_core).wait_recv()
     gt[1] = gram_of(1, 0)
-    for q in (7, 6, 5, 4):
+    for q in (4, 5, 6, 7):
         copy_rows(1, q).wait_recv()
     gt[1] += gram_of(1, 4)
     copy_gs = lambda k: remote(gt.at[k, 1 - s], gr.at[k], gs_sem, (k,), to_core)
     copy_gs(1).start()
-    for q in (7, 6, 5, 4):
+    for q in (4, 5, 6, 7):
         copy_rows(0, q).wait_recv()
     gt[0] += gram_of(0, 4)
     copy_gs(0).start()
@@ -159,16 +171,13 @@
 
     def panel(d, yr, xr):
         g_all = g_bf[...].reshape(2 * half, g_bf.shape[2])
-        return contract1(w_rows(chunk((z + d) % 4, yr, xr)), g_all)
+        return contract1(w_rows(chunk(z_of(d), yr, xr)), g_all)
 
     copy_a1 = lambda yr, d: remote(sa1.at[yr, d], ra1.at[yr, d], a1_sem, (yr, d), to_x)
     copy_b1 = lambda xr, d: remote(sb1.at[xr, d], rb1.at[xr, d], b1_sem, (xr, d), to_y)
     copy_a2 = lambda d: remote(sa2.at[d], ra2.at[d], a2_sem, (d,), to_y)
     copy_b2 = lambda d: remote(sb2.at[d], rb2.at[d], b2_sem, (d,), to_x)
     copy_z = lambda d: remote(s3.at[d], r3.at[d], z_sem, (d,), to_z(d))
-
-    def over_z(step):
-        lax.fori_loop(0, 4, lambda i, carry: (step((i + 1) % 4), carry)[1], 0)
 
     def both_far(d):
         value = panel(d, 1, 1)
@@ -207,21 +216,36 @@
         last = p3[d, :, half:] + rb1[0, d].astype(F32) + rb2[d].astype(F32)
         return first, last
 
-    def third_send(i, carry):
-        d = i + 1
+    def third_send(d):
         first, last = third(d)
         s3[d, 0] = first.astype(BF16)
         s3[d, 1] = last.astype(BF16)
         copy_z(d).start()
-        return carry
-
-    over_z(both_far)
-    over_z(one_far)
-    over_z(near)
-    over_z(second)
-    lax.fori_loop(0, 3, third_send, 0)
+
+    def turn(t):
+        return jnp.where(t < 2, t + 2, 3 - t)
+
+    def sum_step(t, carry):
+        @pl.when(t < 4)
+        def _():
+            d = turn(t)
+            both_far(d)
+            one_far(d)
+            near(d)
+
+        @pl.when(t >= 1)
+        def _():
+            second(turn(t - 1))
+
+        @pl.when(t >= 2)
+        def _():
+            third_send(turn(t - 2))
+
+        return carry
+
+    lax.fori_loop(0, 5, sum_step, 0)
     first, last = third(0)
-    for d in (1, 2, 3):
+    for d in (2, 3, 1):
         copy_z(d).wait_recv()
         first += r3[d, 0].astype(F32)
         last += r3[d, 1].astype(F32)
@@ -231,7 +255,7 @@
     gath[e, 1] = last.astype(BF16)
 
     def held(d, yr, xr):
-        return chunk((z + 4 - d) % 4, yr, xr)
+        return chunk(z_of(d), yr, xr)
 
     def pass_on(c, part, sem, at, where):
         return remote(gath.at[c, part], gath.at[c, part], sem, at, where)
@@ -258,7 +282,7 @@
     def came_b2(xr, d):
         return pass_on(held(d, 1, xr), 1, gb2_sem, (xr, d), to_y)
 
-    for d in (2, 1, 3):
+    for d in (1, 2, 3):
         copy_gz(d).start()
     coef[...] = jnp.zeros_like(coef)
 
@@ -275,32 +299,32 @@
         copy_ga2(0, d).start()
         copy_gb2(0, d).start()
 
-    hand_out(0)
-
-    def forward(d):
+    def take_near(d):
+        came_b2(0, d).wait_recv()
+        add_coef(held(d, 1, 0))
+        came_a2(0, d).wait_recv()
+        add_coef(held(d, 0, 1))
+
+    def gather_step(d, carry):
+        @pl.when(d >= 1)
+        def _():
+            came_z(d).wait_recv()
+
+        hand_out(d)
+        add_coef(held(d, 0, 0))
         came_a1(d).wait_recv()
         copy_ga2(1, d).start()
         came_b1(d).wait_recv()
         copy_gb2(1, d).start()
-        add_coef(held(d, 0, 0))
-
-    def from_z(i, carry):
-        came_z(i + 1).wait_recv()
-        hand_out(i + 1)
-        forward(i)
-        return carry
-
-    lax.fori_loop(0, 3, from_z, 0)
-    forward(3)
-
-    def take_near(d, carry):
-        came_b2(0, d).wait_recv()
-        add_coef(held(d, 1, 0))
-        came_a2(0, d).wait_recv()
-        add_coef(held(d, 0, 1))
-        return carry
-
-    lax.fori_loop(0, 4, take_near, 0)
+
+        @pl.when(d >= 1)
+        def _():
+            take_near(d - 1)
+
+        return carry
+
+    lax.fori_loop(0, 4, gather_step, 0)
+    take_near(3)
 
     def take_far(d, carry):
         came_a2(1, d).wait_recv()
@@ -351,9 +375,10 @@
             jax.ShapeDtypeStruct((rows, cols), F32),
             jax.ShapeDtypeStruct((cols, width // 2), F32),
         ),
-        in_specs=[pl.BlockSpec(memory_space=pl.ANY)] * 2 + [pl.BlockSpec(memory_space=vmem)] * 2,
+        in_specs=[pl.BlockSpec(memory_space=pl.ANY)] * 3 + [pl.BlockSpec(memory_space=vmem)],
         out_specs=[pl.BlockSpec(memory_space=vmem)] * 2,
         scratch_shapes=[
+            vmem(tokens.shape, BF16),
             vmem((depth, width), BF16),
             vmem((depth, cols), BF16),
             vmem((2, 8, cap, width), BF16),
@@ -382,7 +407,7 @@
             vmem((16, 2, rows, half), BF16),
             vmem((2, cols, width // 2), F32),
             vmem((cols, width // 2), F32),
-            dma((2,)),
+            dma((3,)),
             dma((2, 2, 8)),
             dma((2,)),
             dma((2,)),
@@ -408,7 +433,7 @@
         cost_estimate=pl.CostEstimate(
             flops=8 * depth * width * cols, bytes_accessed=2 * depth * width, transcendentals=0
         ),
-    )(weight, probe, ids, tokens)
+    )(weight, probe, tokens, ids)
 
 
 def body(hidden_rows, routes, down_weight, probe):

time: 108 us -> 103 us (0.954); the launches traced: 106 us -> 103 us
  Pallas kernels: 102 us -> 99 us
    pallas_call x1, Pallas kernels: 102 us -> 99 us  [panel_call(): pl.pallas_call(functools.partial(panel_kernel, row_mean), out_shape=(jax....]
where the time goes in v3:
time: 103 us
  Pallas kernels  99 us (96%)
  local copies, waits for them, and re-layouts  3.56 us (3%)
    pallas_call x1, Pallas kernels, panel_call(): pl.pallas_call(functools.partial(panel_kernel, row_mean), out_shape=(jax....  99 us
    unnamed x5, local copies, waits for them, and re-layouts  3.47 us

profile of v3, /device:TPU:0, one launch (start us, length us, event | category | flops | bytes accessed | tf_op | source)
XLA Modules:
  0.0 103.2 jit_solution(155760958208801959)
XLA Ops:
  0.6 0.8 copy.7
  1.4 0.1 reshape.11.ids
  1.5 0.0 copy-start
  1.5 1.2 %copy-done = bf16[64,8,1024]{2,1,0:T(8,128)(2,1)S(1)} copy-done((bf16[64,8,1024]{2,1,0:T(8,128)(2,1)S(1)}, bf16[64,8,1024]{2,1,0:T(8,128)(2,1)}, u32[]{:S(2)}) %copy-start) | copy-done | bytes 1048600
  2.7 99.0 %shard_map.59 = (f32[224,256]{1,0:T(8,128)S(1)}, f32[256,512]{1,0:T(8,128)S(1)}) custom-call(bf16[3584,1024]{1,0:T(8,128)(2,1)} %bitcast.5, bf16[3584,256]{1,0:T(8,128)(2,1)} %probe_any.1, bf16[512,1024]{1,0:T(8,128)(2,1)S(1)} %bitcast.4, s32[1,512]{1,0:T(1,128)S(1)} %reshape.11.ids), custom_call_target="tpu_custom_call" | custom-call | flops 7516192768 | bytes 7340032 | tf_op jit(solution)/shard_map/pallas_call | solution.py:372
  101.7 0.7 copy.10
  102.4 0.8 copy.11
Async XLA Ops:
  1.5 1.2 %copy-start = (bf16[64,8,1024]{2,1,0:T(8,128)(2,1)S(1)}, bf16[64,8,1024]{2,1,0:T(8,128)(2,1)}, u32[]{:S(2)}) copy-start(bf16[64,8,1024]{2,1,0:T(8,128)(2,1)} %param.4) | copy-start | bytes 3145732

commit v4 on v3

--- a/solution.py
+++ b/solution.py
@@ -21,9 +21,9 @@
 
 
 def panel_kernel(
-    row_mean, w_any, probe_any, tokens_any, ids, basis_out, coef_out,
+    row_mean, w_any, probe_any, tokens_any, routes, basis_out, coef_out,
     tokens, w, probe, sent, arr, p_part, p_recv, pt, gt, gr, sp, rp, g_bf, sa1, sb1, ra1, rb1, pa2, pb2, p3, sa2, sb2, ra2, rb2, s3, r3, gath, coef, c_recv,
-    load_sem, rows_sem, p_sem, px_sem, pf_sem, gs_sem, gx_sem, gf_sem, a1_sem, b1_sem, a2_sem, b2_sem, z_sem, gz_sem, ga1_sem, gb1_sem, ga2_sem, gb2_sem, c_sem,
+    load_sem, rows_sem, p_sem, px_sem, po_sem, pf_sem, gs_sem, gx_sem, gf_sem, a1_sem, b1_sem, a2_sem, b2_sem, z_sem, gz_sem, ga1_sem, gb1_sem, ga2_sem, gb2_sem, c_sem,
 ):
     e, s = lax.axis_index("expert"), lax.axis_index("seq")
     x, y, z = e % 2, (e // 2) % 2, e // 4
@@ -51,7 +51,7 @@
             device_id=where, device_id_type=MESH,
         )
 
-    cap = tokens.shape[0] // 8
+    top, cap = routes.shape
     own_half = z // 2
     partner = {"expert": (e + 8) % 16}
 
@@ -75,7 +75,14 @@
         pl.semaphore_signal(barrier, inc=1, device_id=where, device_id_type=MESH)
 
     amount = tokens.shape[0]
-    names = ids[...]
+    lane = lax.broadcasted_iota(jnp.int32, (cap, amount), 1)
+    token = lax.broadcasted_iota(jnp.int32, (cap, amount), 0)
+    inside = lane - token * top
+    widen = jnp.where((inside >= 0) & (inside < top), 1.0, 0.0).astype(BF16)
+    wide = jnp.dot(routes[...].astype(F32).astype(BF16), widen, preferred_element_type=F32)
+    turn_at = lax.rem(lax.broadcasted_iota(jnp.int32, (top, amount), 1), top)
+    line_at = lax.broadcasted_iota(jnp.int32, (top, amount), 0)
+    names = jnp.sum(jnp.where(turn_at == line_at, wide, 0.0), axis=0, keepdims=True).astype(jnp.int32)
     mark = (lax.broadcasted_iota(jnp.int32, (16, amount), 0) == names).astype(F32)
     before = (
         lax.broadcasted_iota(jnp.int32, (amount, amount), 0)
@@ -118,20 +125,23 @@
     load_probe.wait()
     load_w.wait()
     p_part[...] = jnp.zeros_like(p_part)
-    part = 256
+    part = 512
 
     def project(i, carry):
         at = pl.ds(pl.multiple_of(i * part, part), part)
-        p_part[...] += contract0(probe[at, :], w[at, :])
+        p_part[...] += contract0(probe[at, :], w[at, :]).reshape(p_part.shape)
         return carry
 
     lax.fori_loop(0, w.shape[0] // part, project, 0)
-    swap = remote(p_part, p_recv, p_sem, (), to_core)
+    swap = remote(p_part.at[1 - s], p_recv, p_sem, (), to_core)
     swap.start()
-    swap.wait()
-    pt[0] = (p_part[...] + p_recv[...]).astype(BF16).reshape(pt.shape[1:])
+    swap.wait_recv()
+    pt[0, s] = (p_part[s] + p_recv[...]).astype(BF16)
     across = remote(pt.at[0, s], pt.at[1, s], px_sem, (), partner)
     across.start()
+    own = remote(pt.at[0, s], pt.at[0, s], po_sem, (), to_core)
+    own.start()
+    remote(pt.at[0, 1 - s], pt.at[0, 1 - s], po_sem, (), to_core).wait_recv()
 
     def gram_of(k, first):
         rows_k = arr[k, first:first + 4].reshape(4 * cap, arr.shape[3])
@@ -152,107 +162,110 @@
     for q in (4, 5, 6, 7):
         copy_rows(1, q).wait_recv()
     gt[1] += gram_of(1, 4)
-    copy_gs = lambda k: remote(gt.at[k, 1 - s], gr.at[k], gs_sem, (k,), to_core)
-    copy_gs(1).start()
+    copy_gs = lambda k, g: remote(gt.at[k, g, 1 - s], gr.at[k, g], gs_sem, (k, g), to_core)
+    cross = lambda g: remote(sp.at[g], rp.at[g], gx_sem, (g,), partner)
+    spread = lambda g: remote(g_bf.at[g, s], g_bf.at[g, s], gf_sem, (g,), to_core)
+    for g in (0, 1):
+        copy_gs(1, g).start()
+    for g in (0, 1):
+        copy_gs(1, g).wait_recv()
+        sp[g] = (gt[1, g, s] + gr[1, g]).astype(BF16)
+        cross(g).start()
     for q in (4, 5, 6, 7):
         copy_rows(0, q).wait_recv()
     gt[0] += gram_of(0, 4)
-    copy_gs(0).start()
-    copy_gs(1).wait_recv()
-    sp[...] = (gt[1, s] + gr[1]).astype(BF16)
-    cross = remote(sp, rp, gx_sem, (), partner)
-    cross.start()
-    copy_gs(0).wait_recv()
-    cross.wait_recv()
-    g_bf[s] = ((gt[0, s] + gr[0] + rp[...].astype(F32)) / row_mean).astype(BF16)
-    spread = remote(g_bf.at[s], g_bf.at[s], gf_sem, (), to_core)
-    spread.start()
-    remote(g_bf.at[1 - s], g_bf.at[1 - s], gf_sem, (), to_core).wait_recv()
-
-    def panel(d, yr, xr):
-        g_all = g_bf[...].reshape(2 * half, g_bf.shape[2])
-        return contract1(w_rows(chunk(z_of(d), yr, xr)), g_all)
-
-    copy_a1 = lambda yr, d: remote(sa1.at[yr, d], ra1.at[yr, d], a1_sem, (yr, d), to_x)
-    copy_b1 = lambda xr, d: remote(sb1.at[xr, d], rb1.at[xr, d], b1_sem, (xr, d), to_y)
-    copy_a2 = lambda d: remote(sa2.at[d], ra2.at[d], a2_sem, (d,), to_y)
-    copy_b2 = lambda d: remote(sb2.at[d], rb2.at[d], b2_sem, (d,), to_x)
-    copy_z = lambda d: remote(s3.at[d], r3.at[d], z_sem, (d,), to_z(d))
-
-    def both_far(d):
-        value = panel(d, 1, 1)
-        sa1[1, d] = value[:, :half].astype(BF16)
-        copy_a1(1, d).start()
-        sb1[1, d] = value[:, half:].astype(BF16)
-        copy_b1(1, d).start()
-
-    def one_far(d):
-        value = panel(d, 0, 1)
-        sa1[0, d] = value[:, :half].astype(BF16)
-        copy_a1(0, d).start()
-        pb2[d] = value[:, half:]
-        value = panel(d, 1, 0)
-        sb1[0, d] = value[:, half:].astype(BF16)
-        copy_b1(0, d).start()
-        pa2[d] = value[:, :half]
-
-    def near(d):
-        p3[d] = panel(d, 0, 0)
-
-    def second(d):
-        copy_a1(1, d).wait_recv()
-        sa2[d] = (pa2[d] + ra1[1, d].astype(F32)).astype(BF16)
-        copy_a2(d).start()
-        copy_b1(1, d).wait_recv()
-        sb2[d] = (pb2[d] + rb1[1, d].astype(F32)).astype(BF16)
-        copy_b2(d).start()
-
-    def third(d):
-        copy_a1(0, d).wait_recv()
-        copy_a2(d).wait_recv()
-        first = p3[d, :, :half] + ra1[0, d].astype(F32) + ra2[d].astype(F32)
-        copy_b1(0, d).wait_recv()
-        copy_b2(d).wait_recv()
-        last = p3[d, :, half:] + rb1[0, d].astype(F32) + rb2[d].astype(F32)
-        return first, last
-
-    def third_send(d):
-        first, last = third(d)
-        s3[d, 0] = first.astype(BF16)
-        s3[d, 1] = last.astype(BF16)
-        copy_z(d).start()
-
-    def turn(t):
-        return jnp.where(t < 2, t + 2, 3 - t)
+    for g in (0, 1):
+        copy_gs(0, g).start()
+
+    def finish_gram(g):
+        copy_gs(0, g).wait_recv()
+        cross(g).wait_recv()
+        total = gt[0, g, s] + gr[0, g] + rp[g].astype(F32)
+        g_bf[g, s] = (total / row_mean).astype(BF16)
+        spread(g).start()
+        remote(g_bf.at[g, 1 - s], g_bf.at[g, 1 - s], gf_sem, (g,), to_core).wait_recv()
+
+    finish_gram(0)
+
+    part = rows // 2
+
+    def panel(g, d, yr, xr):
+        return contract1(w_rows(chunk(z_of(d), yr, xr)), g_bf[g].reshape(half, g_bf.shape[3]))
+
+    copy_a1 = lambda g, yr, d: remote(sa1.at[g, yr, d], ra1.at[g, yr, d], a1_sem, (g, yr, d), to_x)
+    copy_b1 = lambda g, xr, d: remote(sb1.at[g, xr, d], rb1.at[g, xr, d], b1_sem, (g, xr, d), to_y)
+    copy_a2 = lambda g, d: remote(sa2.at[g, d], ra2.at[g, d], a2_sem, (g, d), to_y)
+    copy_b2 = lambda g, d: remote(sb2.at[g, d], rb2.at[g, d], b2_sem, (g, d), to_x)
+    copy_z = lambda g, d: remote(s3.at[g, d], r3.at[g, d], z_sem, (g, d), to_z(d))
+
+    def first_stage(g, d):
+        value = panel(g, d, 1, 1)
+        sa1[g, 1, d] = value[:part].astype(BF16)
+        copy_a1(g, 1, d).start()
+        sb1[g, 1, d] = value[part:].astype(BF16)
+        copy_b1(g, 1, d).start()
+        value = panel(g, d, 0, 1)
+        sa1[g, 0, d] = value[:part].astype(BF16)
+        copy_a1(g, 0, d).start()
+        pb2[g, d] = value[part:]
+        value = panel(g, d, 1, 0)
+        sb1[g, 0, d] = value[part:].astype(BF16)
+        copy_b1(g, 0, d).start()
+        pa2[g, d] = value[:part]
+        p3[g, d] = panel(g, d, 0, 0)
+
+    def second_stage(g, d):
+        copy_a1(g, 1, d).wait_recv()
+        sa2[g, d] = (pa2[g, d] + ra1[g, 1, d].astype(F32)).astype(BF16)
+        copy_a2(g, d).start()
+        copy_b1(g, 1, d).wait_recv()
+        sb2[g, d] = (pb2[g, d] + rb1[g, 1, d].astype(F32)).astype(BF16)
+        copy_b2(g, d).start()
+
+    def third_stage(g, d):
+        copy_a1(g, 0, d).wait_recv()
+        copy_a2(g, d).wait_recv()
+        p3[g, d, :part] += ra1[g, 0, d].astype(F32) + ra2[g, d].astype(F32)
+        copy_b1(g, 0, d).wait_recv()
+        copy_b2(g, d).wait_recv()
+        p3[g, d, part:] += rb1[g, 0, d].astype(F32) + rb2[g, d].astype(F32)
+
+        @pl.when(d != 0)
+        def _():
+            s3[g, d] = p3[g, d].astype(BF16).reshape(s3.shape[2:])
+            copy_z(g, d).start()
+
+    def item(t):
+        i = t % 4
+        return t // 4, jnp.where(i < 2, i + 2, 3 - i)
 
     def sum_step(t, carry):
-        @pl.when(t < 4)
-        def _():
-            d = turn(t)
-            both_far(d)
-            one_far(d)
-            near(d)
-
-        @pl.when(t >= 1)
-        def _():
-            second(turn(t - 1))
+        @pl.when(t == 4)
+        def _():
+            finish_gram(1)
+
+        @pl.when(t < 8)
+        def _():
+            first_stage(*item(t))
+
+        @pl.when((t >= 1) & (t < 9))
+        def _():
+            second_stage(*item(t - 1))
 
         @pl.when(t >= 2)
         def _():
-            third_send(turn(t - 2))
+            third_stage(*item(t - 2))
 
         return carry
 
-    lax.fori_loop(0, 5, sum_step, 0)
-    first, last = third(0)
-    for d in (2, 3, 1):
-        copy_z(d).wait_recv()
-        first += r3[d, 0].astype(F32)
-        last += r3[d, 1].astype(F32)
-    basis_out[:, :half] = first
-    basis_out[:, half:] = last
-    gath[e, 0] = first.astype(BF16)
-    gath[e, 1] = last.astype(BF16)
+    lax.fori_loop(0, 10, sum_step, 0)
+    for g in (0, 1):
+        total = p3[g, 0]
+        for d in (2, 3, 1):
+            copy_z(g, d).wait_recv()
+            total += r3[g, d].astype(F32).reshape(rows, half)
+        basis_out[:, g * half:(g + 1) * half] = total
+        gath[e, :, :, g * half:(g + 1) * half] = total.astype(BF16).reshape(2, part, half)
 
     def held(d, yr, xr):
         return chunk(z_of(d), yr, xr)
@@ -287,7 +300,7 @@
     coef[...] = jnp.zeros_like(coef)
 
     def add_coef(c):
-        block = jnp.concatenate([gath[c, 0], gath[c, 1]], axis=1)
+        block = gath[c].reshape(rows, gath.shape[3])
         value = contract0(block, w_rows(c))
         width = value.shape[1] // 2
         coef[0] += value[:, :width]
@@ -339,34 +352,40 @@
 
     def drain(d, carry):
         for k in (0, 1):
-            copy_a1(k, d).wait_send()
-            copy_b1(k, d).wait_send()
+            for g in (0, 1):
+                copy_a1(g, k, d).wait_send()
+                copy_b1(g, k, d).wait_send()
+            copy_a2(k, d).wait_send()
+            copy_b2(k, d).wait_send()
             copy_ga2(k, d).wait_send()
             copy_gb2(k, d).wait_send()
-        copy_a2(d).wait_send()
-        copy_b2(d).wait_send()
         copy_ga1(d).wait_send()
         copy_gb1(d).wait_send()
         return carry
 
     lax.fori_loop(0, 4, drain, 0)
     for d in (1, 2, 3):
-        copy_z(d).wait_send()
+        copy_z(0, d).wait_send()
+        copy_z(1, d).wait_send()
         copy_gz(d).wait_send()
     for q in range(1, 8):
         copy_rows(0, q).wait_send()
         copy_rows(1, q).wait_send()
-    for copy in (across, hand, copy_gs(0), copy_gs(1), cross, spread):
+    for copy in (swap, across, own, hand):
         copy.wait_send()
+    for g in (0, 1):
+        for copy in (copy_gs(0, g), copy_gs(1, g), cross(g), spread(g)):
+            copy.wait_send()
     share.wait()
     coef_out[...] = coef[s] + c_recv[...]
 
 
-def panel_call(weight, probe, ids, tokens, row_mean):
+def panel_call(weight, probe, routes, tokens, row_mean):
     depth, width = weight.shape
     cols = probe.shape[1]
-    cap = tokens.shape[0] // 8
+    cap = routes.shape[1]
     rows, half = depth // 16, cols // 2
+    part, quarter = rows // 2, half // 2
     dma = pltpu.SemaphoreType.DMA
     vmem = pltpu.VMEM
     return pl.pallas_call(
@@ -383,28 +402,28 @@
             vmem((depth, cols), BF16),
             vmem((2, 8, cap, width), BF16),
             vmem((2, 8, cap, width), BF16),
-            vmem((cols, width), F32),
-            vmem((cols, width), F32),
+            vmem((2, half, width), F32),
+            vmem((half, width), F32),
             vmem((2, 2, half, width), BF16),
-            vmem((2, 2, half, width), F32),
-            vmem((2, half, width), F32),
-            vmem((half, width), BF16),
-            vmem((half, width), BF16),
-            vmem((2, half, width), BF16),
-            vmem((2, 4, rows, half), BF16),
-            vmem((2, 4, rows, half), BF16),
-            vmem((2, 4, rows, half), BF16),
-            vmem((2, 4, rows, half), BF16),
-            vmem((4, rows, half), F32),
-            vmem((4, rows, half), F32),
-            vmem((4, rows, cols), F32),
-            vmem((4, rows, half), BF16),
-            vmem((4, rows, half), BF16),
-            vmem((4, rows, half), BF16),
-            vmem((4, rows, half), BF16),
-            vmem((4, 2, rows, half), BF16),
-            vmem((4, 2, rows, half), BF16),
-            vmem((16, 2, rows, half), BF16),
+            vmem((2, 2, 2, quarter, width), F32),
+            vmem((2, 2, quarter, width), F32),
+            vmem((2, quarter, width), BF16),
+            vmem((2, quarter, width), BF16),
+            vmem((2, 2, quarter, width), BF16),
+            vmem((2, 2, 4, part, half), BF16),
+            vmem((2, 2, 4, part, half), BF16),
+            vmem((2, 2, 4, part, half), BF16),
+            vmem((2, 2, 4, part, half), BF16),
+            vmem((2, 4, part, half), F32),
+            vmem((2, 4, part, half), F32),
+            vmem((2, 4, rows, half), F32),
+            vmem((2, 4, part, half), BF16),
+            vmem((2, 4, part, half), BF16),
+            vmem((2, 4, part, half), BF16),
+            vmem((2, 4, part, half), BF16),
+            vmem((2, 4, 2, part, half), BF16),
+            vmem((2, 4, 2, part, half), BF16),
+            vmem((16, 2, part, cols), BF16),
             vmem((2, cols, width // 2), F32),
             vmem((cols, width // 2), F32),
             dma((3,)),
@@ -412,14 +431,15 @@
             dma((2,)),
             dma((2,)),
             dma((2,)),
+            dma((2,)),
+            dma((2, 2, 2)),
             dma((2, 2)),
-            dma((2,)),
-            dma((2,)),
+            dma((2, 2)),
+            dma((2, 2, 2, 4)),
+            dma((2, 2, 2, 4)),
             dma((2, 2, 4)),
             dma((2, 2, 4)),
-            dma((2, 4)),
-            dma((2, 4)),
-            dma((2, 4)),
+            dma((2, 2, 4)),
             dma((2, 4)),
             dma((2, 4)),
             dma((2, 4)),
@@ -428,12 +448,12 @@
             dma((2,)),
         ],
         compiler_params=pltpu.CompilerParams(
-            collective_id=0, has_side_effects=True, vmem_limit_bytes=52 * 2**20
+            collective_id=0, has_side_effects=True, vmem_limit_bytes=127 * 2**19
         ),
         cost_estimate=pl.CostEstimate(
             flops=8 * depth * width * cols, bytes_accessed=2 * depth * width, transcendentals=0
         ),
-    )(weight, probe, tokens, ids)
+    )(weight, probe, tokens, routes)
 
 
 def body(hidden_rows, routes, down_weight, probe):
@@ -444,9 +464,8 @@
     capacity = 2 * tok_count * top_count // experts
     row_mean = tok_count * top_count * lax.axis_size("seq")
     if experts == 16 and lax.axis_size("seq") == 2:
-        ids = routes.reshape(1, -1)
         tokens = hidden_rows.reshape(-1, feature_width)
-        basis_rows, coefficients = panel_call(weight, probe, ids, tokens, row_mean)
+        basis_rows, coefficients = panel_call(weight, probe, routes.T, tokens, row_mean)
         return (basis_rows, coefficients[None])
     partial_value = lax.dot_general(
         weight, probe, (((0,), (0,)), ((), ())), preferred_element_type=jnp.float32

time: 103 us -> 105 us (1.019)
  Pallas kernels: 99 us -> 101 us
    pallas_call x1, Pallas kernels: 99 us -> 101 us  [panel_call(): pl.pallas_call(functools.partial(panel_kernel, row_mean), out_shape=(jax....]
    unnamed x5 -> x2, local copies, waits for them, and re-layouts: 3.47 us -> 3.51 us
where the time goes in v4:
time: 105 us
  Pallas kernels  101 us (96%)
  local copies, waits for them, and re-layouts  3.51 us (3%)
    pallas_call x1, Pallas kernels, panel_call(): pl.pallas_call(functools.partial(panel_kernel, row_mean), out_shape=(jax....  101 us
    unnamed x2, local copies, waits for them, and re-layouts  3.51 us

profile of v4, /device:TPU:0, one launch (start us, length us, event | category | flops | bytes accessed | tf_op | source)
XLA Modules:
  0.0 105.2 jit_solution(14715765946703011477)
XLA Ops:
  0.6 101.0 %shard_map.59 = (f32[224,256]{1,0:T(8,128)}, f32[256,512]{1,0:T(8,128)}) custom-call(bf16[3584,1024]{1,0:T(8,128)(2,1)} %bitcast.5, bf16[3584,256]{1,0:T(8,128)(2,1)} %probe_any.1, bf16[512,1024]{1,0:T(8,128)(2,1)} %bitcast.6, s32[8,64]{1,0:T(8,128)} %bitcast.7), custom_call_target="tpu_custom_call" | custom-call | flops 7516192768 | bytes 7340032 | tf_op jit(solution)/shard_map/pallas_call | solution.py:391
  101.6 1.6 %copy.8 = f32[224,256]{1,0:T(8,128)} copy(f32[224,256]{1,0:T(8,128)} %get-tuple-element.8) | data formatting | bytes 458752
  103.3 1.9 %copy.9 = f32[1,256,512]{2,1,0:T(8,128)} copy(f32[1,256,512]{2,1,0:T(8,128)} %bitcast.4) | data formatting | bytes 1048576

commit v5 on v4

--- a/solution.py
+++ b/solution.py
@@ -22,7 +22,7 @@
 
 def panel_kernel(
     row_mean, w_any, probe_any, tokens_any, routes, basis_out, coef_out,
-    tokens, w, probe, sent, arr, p_part, p_recv, pt, gt, gr, sp, rp, g_bf, sa1, sb1, ra1, rb1, pa2, pb2, p3, sa2, sb2, ra2, rb2, s3, r3, gath, coef, c_recv,
+    tokens, w, probe, sent, arr, p_part, p_recv, pt, gt, gr, sp, rp, g_bf, sa1, sb1, ra1, rb1, pa2, pb2, whole, p3, sa2, sb2, ra2, rb2, s3, r3, gath, coef, c_recv,
     load_sem, rows_sem, p_sem, px_sem, po_sem, pf_sem, gs_sem, gx_sem, gf_sem, a1_sem, b1_sem, a2_sem, b2_sem, z_sem, gz_sem, ga1_sem, gb1_sem, ga2_sem, gb2_sem, c_sem,
 ):
     e, s = lax.axis_index("expert"), lax.axis_index("seq")
@@ -98,29 +98,37 @@
         sent.at[k, i], arr.at[k, i], rows_sem, (k, i), {"expert": slot_chip(i)}
     )
 
-    def block_for(i):
-        chip = slot_chip(i)
+    def blocks_for(slots):
         line = lax.broadcasted_iota(jnp.int32, (2 * cap, amount), 0)
-        wanted = jnp.where(line < cap, chip * cap + line, ((chip + 8) % 16 - 1) * cap + line)
-        pick = (wanted == place).astype(F32).astype(BF16)
-        return jnp.dot(pick, tokens[...], preferred_element_type=F32).astype(BF16)
+        picks = []
+        for i in slots:
+            chip = slot_chip(i)
+            wanted = jnp.where(line < cap, chip * cap + line, ((chip + 8) % 16 - 1) * cap + line)
+            picks.append((wanted == place).astype(F32).astype(BF16))
+        pick = jnp.concatenate(picks, axis=0)
+        found = jnp.dot(pick, tokens[...], preferred_element_type=F32).astype(BF16)
+        return found.reshape(len(slots), 2, cap, found.shape[1])
 
     load_tokens.wait()
     pl.semaphore_wait(barrier, 10)
 
-    def send_rows(j, carry):
-        i = j + 1
-        block = block_for(i)
-        sent[0, i] = block[:cap]
-        copy_rows(0, i).start()
-        sent[1, i] = block[cap:]
-        copy_rows(1, i).start()
+    def send_rows(i, block):
+        for k in (0, 1):
+            sent[k, i] = block[k]
+            copy_rows(k, i).start()
+
+    def send_pair(j, carry):
+        i = 2 * j + 1
+        blocks = blocks_for((i, i + 1))
+        send_rows(i, blocks[0])
+        send_rows(i + 1, blocks[1])
         return carry
 
-    lax.fori_loop(0, 7, send_rows, 0)
-    block = block_for(0)
-    arr[0, 0] = block[:cap]
-    arr[1, 0] = block[cap:]
+    lax.fori_loop(0, 3, send_pair, 0)
+    blocks = blocks_for((7, 0))
+    send_rows(7, blocks[0])
+    arr[0, 0] = blocks[1, 0]
+    arr[1, 0] = blocks[1, 1]
 
     load_probe.wait()
     load_w.wait()
@@ -189,9 +197,6 @@
 
     part = rows // 2
 
-    def panel(g, d, yr, xr):
-        return contract1(w_rows(chunk(z_of(d), yr, xr)), g_bf[g].reshape(half, g_bf.shape[3]))
-
     copy_a1 = lambda g, yr, d: remote(sa1.at[g, yr, d], ra1.at[g, yr, d], a1_sem, (g, yr, d), to_x)
     copy_b1 = lambda g, xr, d: remote(sb1.at[g, xr, d], rb1.at[g, xr, d], b1_sem, (g, xr, d), to_y)
     copy_a2 = lambda g, d: remote(sa2.at[g, d], ra2.at[g, d], a2_sem, (g, d), to_y)
@@ -199,20 +204,24 @@
     copy_z = lambda g, d: remote(s3.at[g, d], r3.at[g, d], z_sem, (g, d), to_z(d))
 
     def first_stage(g, d):
-        value = panel(g, d, 1, 1)
-        sa1[g, 1, d] = value[:part].astype(BF16)
+        at = pl.ds(pl.multiple_of(z_of(d) * 4 * rows, rows), 4 * rows)
+        value = contract1(w[at, :], g_bf[g].reshape(half, g_bf.shape[3]))
+        whole[...] = value.reshape(whole.shape)
+        place_of = lambda yr, xr: (y + yr) % 2 * 2 + (x + xr) % 2
+        c = place_of(1, 1)
+        sa1[g, 1, d] = whole[c, 0].astype(BF16)
         copy_a1(g, 1, d).start()
-        sb1[g, 1, d] = value[part:].astype(BF16)
+        sb1[g, 1, d] = whole[c, 1].astype(BF16)
         copy_b1(g, 1, d).start()
-        value = panel(g, d, 0, 1)
-        sa1[g, 0, d] = value[:part].astype(BF16)
+        c = place_of(0, 1)
+        sa1[g, 0, d] = whole[c, 0].astype(BF16)
         copy_a1(g, 0, d).start()
-        pb2[g, d] = value[part:]
-        value = panel(g, d, 1, 0)
-        sb1[g, 0, d] = value[part:].astype(BF16)
+        pb2[g, d] = whole[c, 1]
+        c = place_of(1, 0)
+        sb1[g, 0, d] = whole[c, 1].astype(BF16)
         copy_b1(g, 0, d).start()
-        pa2[g, d] = value[:part]
-        p3[g, d] = panel(g, d, 0, 0)
+        pa2[g, d] = whole[c, 0]
+        p3[g, d] = whole[place_of(0, 0)].reshape(rows, half)
 
     def second_stage(g, d):
         copy_a1(g, 1, d).wait_recv()
@@ -314,9 +323,21 @@
 
     def take_near(d):
         came_b2(0, d).wait_recv()
-        add_coef(held(d, 1, 0))
         came_a2(0, d).wait_recv()
-        add_coef(held(d, 0, 1))
+
+    def take_far(d):
+        came_a2(1, d).wait_recv()
+        came_b2(1, d).wait_recv()
+
+    def add_whole(d):
+        take_near(d)
+        take_far(d)
+        first = z_of(d) * 4
+        block = gath[pl.ds(first, 4)].reshape(4 * rows, gath.shape[3])
+        value = contract0(block, w[pl.ds(pl.multiple_of(first * rows, rows), 4 * rows), :])
+        width = value.shape[1] // 2
+        coef[0] += value[:, :width]
+        coef[1] += value[:, width:]
 
     def gather_step(d, carry):
         @pl.when(d >= 1)
@@ -324,28 +345,25 @@
             came_z(d).wait_recv()
 
         hand_out(d)
-        add_coef(held(d, 0, 0))
+
+        @pl.when(d >= 2)
+        def _():
+            add_whole(d - 2)
+
         came_a1(d).wait_recv()
         copy_ga2(1, d).start()
         came_b1(d).wait_recv()
         copy_gb2(1, d).start()
-
-        @pl.when(d >= 1)
-        def _():
-            take_near(d - 1)
-
         return carry
 
     lax.fori_loop(0, 4, gather_step, 0)
+    add_coef(held(3, 0, 0))
+    add_whole(2)
     take_near(3)
-
-    def take_far(d, carry):
-        came_a2(1, d).wait_recv()
-        came_b2(1, d).wait_recv()
-        add_coef(held(d, 1, 1))
-        return carry
-
-    lax.fori_loop(0, 4, take_far, 0)
+    add_coef(held(3, 1, 0))
+    add_coef(held(3, 0, 1))
+    take_far(3)
+    add_coef(held(3, 1, 1))
 
     share = remote(coef.at[1 - s], c_recv, c_sem, (), to_core)
     share.start()
@@ -394,7 +412,7 @@
             jax.ShapeDtypeStruct((rows, cols), F32),
             jax.ShapeDtypeStruct((cols, width // 2), F32),
         ),
-        in_specs=[pl.BlockSpec(memory_space=pl.ANY)] * 3 + [pl.BlockSpec(memory_space=vmem)],
+        in_specs=[pl.BlockSpec(memory_space=pltpu.HBM)] * 3 + [pl.BlockSpec(memory_space=vmem)],
         out_specs=[pl.BlockSpec(memory_space=vmem)] * 2,
         scratch_shapes=[
             vmem(tokens.shape, BF16),
@@ -416,6 +434,7 @@
             vmem((2, 2, 4, part, half), BF16),
             vmem((2, 4, part, half), F32),
             vmem((2, 4, part, half), F32),
+            vmem((4, 2, part, half), F32),
             vmem((2, 4, rows, half), F32),
             vmem((2, 4, part, half), BF16),
             vmem((2, 4, part, half), BF16),
@@ -448,7 +467,7 @@
             dma((2,)),
         ],
         compiler_params=pltpu.CompilerParams(
-            collective_id=0, has_side_effects=True, vmem_limit_bytes=127 * 2**19
+            collective_id=0, has_side_effects=True, vmem_limit_bytes=52 * 2**20
         ),
         cost_estimate=pl.CostEstimate(
             flops=8 * depth * width * cols, bytes_accessed=2 * depth * width, transcendentals=0

time: 105 us -> 103 us (0.981)
  Pallas kernels: 101 us -> 98.9 us
    pallas_call x1, Pallas kernels: 101 us -> 98.9 us  [panel_call(): pl.pallas_call(functools.partial(panel_kernel, row_mean), out_shape=(jax....]
    unnamed x2 -> x6, local copies, waits for them, and re-layouts: 3.51 us -> 3.39 us
where the time goes in v5:
time: 103 us
  Pallas kernels  98.9 us (96%)
  local copies, waits for them, and re-layouts  3.39 us (3%)
    pallas_call x1, Pallas kernels, panel_call(): pl.pallas_call(functools.partial(panel_kernel, row_mean), out_shape=(jax....  98.9 us
    unnamed x6, local copies, waits for them, and re-layouts  3.39 us

profile of v5, /device:TPU:0, one launch (start us, length us, event | category | flops | bytes accessed | tf_op | source)
XLA Modules:
  0.0 103.0 jit_solution(8605955364094586063)
XLA Ops:
  0.6 0.0 copy-start
  0.6 1.2 %copy-done = bf16[64,8,1024]{2,1,0:T(8,128)(2,1)S(1)} copy-done((bf16[64,8,1024]{2,1,0:T(8,128)(2,1)S(1)}, bf16[64,8,1024]{2,1,0:T(8,128)(2,1)}, u32[]{:S(2)}) %copy-start) | copy-done | bytes 1048600
  1.9 0.0 copy-start.1
  1.9 0.7 copy-done.1
  2.5 98.9 %shard_map.59 = (f32[224,256]{1,0:T(8,128)S(1)}, f32[256,512]{1,0:T(8,128)S(1)}) custom-call(bf16[3584,1024]{1,0:T(8,128)(2,1)} %bitcast.7, bf16[3584,256]{1,0:T(8,128)(2,1)} %probe_any.1, bf16[512,1024]{1,0:T(8,128)(2,1)S(1)} %bitcast.5, s32[8,64]{1,0:T(8,128)S(1)} %bitcast.6), custom_call_target="tpu_custom_call" | custom-call | flops 7516192768 | bytes 7340032 | tf_op jit(solution)/shard_map/pallas_call | solution.py:409
  101.5 0.7 copy.8
  102.2 0.8 copy.9
Async XLA Ops:
  0.6 1.2 %copy-start = (bf16[64,8,1024]{2,1,0:T(8,128)(2,1)S(1)}, bf16[64,8,1024]{2,1,0:T(8,128)(2,1)}, u32[]{:S(2)}) copy-start(bf16[64,8,1024]{2,1,0:T(8,128)(2,1)} %param.4) | copy-start | bytes 3145732
  1.9 0.7 copy-start.1

commit v6 on v5

--- a/solution.py
+++ b/solution.py
@@ -175,10 +175,9 @@
     spread = lambda g: remote(g_bf.at[g, s], g_bf.at[g, s], gf_sem, (g,), to_core)
     for g in (0, 1):
         copy_gs(1, g).start()
-    for g in (0, 1):
-        copy_gs(1, g).wait_recv()
-        sp[g] = (gt[1, g, s] + gr[1, g]).astype(BF16)
-        cross(g).start()
+    copy_gs(1, 0).wait_recv()
+    sp[0] = (gt[1, 0, s] + gr[1, 0]).astype(BF16)
+    cross(0).start()
     for q in (4, 5, 6, 7):
         copy_rows(0, q).wait_recv()
     gt[0] += gram_of(0, 4)
@@ -193,6 +192,10 @@
         spread(g).start()
         remote(g_bf.at[g, 1 - s], g_bf.at[g, 1 - s], gf_sem, (g,), to_core).wait_recv()
 
+    copy_gs(1, 1).wait_recv()
+    sp[1] = (gt[1, 1, s] + gr[1, 1]).astype(BF16)
+    cross(0).wait_send()
+    cross(1).start()
     finish_gram(0)
 
     part = rows // 2
@@ -304,8 +307,8 @@
     def came_b2(xr, d):
         return pass_on(held(d, 1, xr), 1, gb2_sem, (xr, d), to_y)
 
-    for d in (1, 2, 3):
-        copy_gz(d).start()
+    copy_gz(1).start()
+    copy_gz(2).start()
     coef[...] = jnp.zeros_like(coef)
 
     def add_coef(c):
@@ -345,6 +348,10 @@
             came_z(d).wait_recv()
 
         hand_out(d)
+
+        @pl.when(d == 1)
+        def _():
+            copy_gz(3).start()
 
         @pl.when(d >= 2)
         def _():
@@ -392,8 +399,9 @@
     for copy in (swap, across, own, hand):
         copy.wait_send()
     for g in (0, 1):
-        for copy in (copy_gs(0, g), copy_gs(1, g), cross(g), spread(g)):
+        for copy in (copy_gs(0, g), copy_gs(1, g), spread(g)):
             copy.wait_send()
+    cross(1).wait_send()
     share.wait()
     coef_out[...] = coef[s] + c_recv[...]
 

time: 103 us -> 103 us (level)
  no operation moved by 1% of the time
where the time goes in v6:
time: 103 us
  Pallas kernels  99.1 us (96%)
  local copies, waits for them, and re-layouts  3.39 us (3%)
    pallas_call x1, Pallas kernels, panel_call(): pl.pallas_call(functools.partial(panel_kernel, row_mean), out_shape=(jax....  99.1 us
    unnamed x6, local copies, waits for them, and re-layouts  3.39 us

profile of v6, /device:TPU:0, one launch (start us, length us, event | category | flops | bytes accessed | tf_op | source)
XLA Modules:
  0.0 103.2 jit_solution(14949746786335025602)
XLA Ops:
  0.6 0.0 copy-start
  0.6 1.2 %copy-done = bf16[64,8,1024]{2,1,0:T(8,128)(2,1)S(1)} copy-done((bf16[64,8,1024]{2,1,0:T(8,128)(2,1)S(1)}, bf16[64,8,1024]{2,1,0:T(8,128)(2,1)}, u32[]{:S(2)}) %copy-start) | copy-done | bytes 1048600
  1.9 0.0 copy-start.1
  1.9 0.7 copy-done.1
  2.5 99.1 %shard_map.59 = (f32[224,256]{1,0:T(8,128)S(1)}, f32[256,512]{1,0:T(8,128)S(1)}) custom-call(bf16[3584,1024]{1,0:T(8,128)(2,1)} %bitcast.7, bf16[3584,256]{1,0:T(8,128)(2,1)} %probe_any.1, bf16[512,1024]{1,0:T(8,128)(2,1)S(1)} %bitcast.5, s32[8,64]{1,0:T(8,128)S(1)} %bitcast.6), custom_call_target="tpu_custom_call" | custom-call | flops 7516192768 | bytes 7340032 | tf_op jit(solution)/shard_map/pallas_call | solution.py:417
  101.7 0.7 copy.8
  102.4 0.8 copy.9
Async XLA Ops:
  0.6 1.2 %copy-start = (bf16[64,8,1024]{2,1,0:T(8,128)(2,1)S(1)}, bf16[64,8,1024]{2,1,0:T(8,128)(2,1)}, u32[]{:S(2)}) copy-start(bf16[64,8,1024]{2,1,0:T(8,128)(2,1)} %param.4) | copy-start | bytes 3145732
  1.9 0.7 copy-start.1

commit v7 on v6

--- a/solution.py
+++ b/solution.py
@@ -252,6 +252,10 @@
         return t // 4, jnp.where(i < 2, i + 2, 3 - i)
 
     def sum_step(t, carry):
+        @pl.when((t >= 2) & (t < 10))
+        def _():
+            second_stage(*item(t - 2))
+
         @pl.when(t == 4)
         def _():
             finish_gram(1)
@@ -260,17 +264,13 @@
         def _():
             first_stage(*item(t))
 
-        @pl.when((t >= 1) & (t < 9))
-        def _():
-            second_stage(*item(t - 1))
-
-        @pl.when(t >= 2)
-        def _():
-            third_stage(*item(t - 2))
+        @pl.when(t >= 4)
+        def _():
+            third_stage(*item(t - 4))
 
         return carry
 
-    lax.fori_loop(0, 10, sum_step, 0)
+    lax.fori_loop(0, 12, sum_step, 0)
     for g in (0, 1):
         total = p3[g, 0]
         for d in (2, 3, 1):
@@ -475,7 +475,7 @@
             dma((2,)),
         ],
         compiler_params=pltpu.CompilerParams(
-            collective_id=0, has_side_effects=True, vmem_limit_bytes=52 * 2**20
+            collective_id=0, has_side_effects=True, vmem_limit_bytes=61072 * 2**10
         ),
         cost_estimate=pl.CostEstimate(
             flops=8 * depth * width * cols, bytes_accessed=2 * depth * width, transcendentals=0

time: 103 us -> 104 us (level)
    unnamed x6 -> x2, local copies, waits for them, and re-layouts: 3.39 us -> 3.51 us
where the time goes in v7:
time: 104 us; the launch traced here: 103 us
  Pallas kernels  99.2 us (95%)
  local copies, waits for them, and re-layouts  3.51 us (3%)
    pallas_call x1, Pallas kernels, panel_call(): pl.pallas_call(functools.partial(panel_kernel, row_mean), out_shape=(jax....  99.2 us
    unnamed x2, local copies, waits for them, and re-layouts  3.51 us

profile of v7, /device:TPU:0, one launch (start us, length us, event | category | flops | bytes accessed | tf_op | source)
XLA Modules:
  0.0 103.3 jit_solution(367452512992411839)
XLA Ops:
  0.6 99.2 %shard_map.59 = (f32[224,256]{1,0:T(8,128)}, f32[256,512]{1,0:T(8,128)}) custom-call(bf16[3584,1024]{1,0:T(8,128)(2,1)} %bitcast.5, bf16[3584,256]{1,0:T(8,128)(2,1)} %probe_any.1, bf16[512,1024]{1,0:T(8,128)(2,1)} %bitcast.6, s32[8,64]{1,0:T(8,128)} %bitcast.7), custom_call_target="tpu_custom_call" | custom-call | flops 7516192768 | bytes 7340032 | tf_op jit(solution)/shard_map/pallas_call | solution.py:417
  99.8 1.6 %copy.8 = f32[224,256]{1,0:T(8,128)} copy(f32[224,256]{1,0:T(8,128)} %get-tuple-element.8) | data formatting | bytes 458752
  101.5 1.9 %copy.9 = f32[1,256,512]{2,1,0:T(8,128)} copy(f32[1,256,512]{2,1,0:T(8,128)} %bitcast.4) | data formatting | bytes 1048576
